TPU v7x, 128 devices: a whole 4x4x4 slice. The times are simulated.
128 devices in a mesh: dp: 4 (over x), ctx: 32 (over z, y, core).
Axes of the slice: x: 4, y: 4, z: 4, core: 2. Of those that a mesh axis runs over, the one named last changes fastest.
Arguments:
- queries: bfloat16 [4, 4096, 4096], P('dp', 'ctx'), may hold values from -9.5 to 9.5
- keys: bfloat16 [4, 4096, 512], P('dp', 'ctx'), may hold values from -6 to 6
- values: bfloat16 [4, 4096, 512], P('dp', 'ctx'), may hold values from -6 to 6
- out_grad: bfloat16 [4, 4096, 4096], P('dp', 'ctx'), may hold values from -6 to 6
- segment_ids: int32 [4, 4096], P('dp', 'ctx'), may hold values from 0 to 3, never falling along the last dimension, each value on 1 to 2048 neighbouring positions
- loss_mask: int32 [4, 4096], P('dp', 'ctx'), may hold values from 0 to 1, as said below
Outputs:
- attn_out: bfloat16 [4, 4096, 4096], P('dp', 'ctx')
- q_grad: bfloat16 [4, 4096, 4096], P('dp', 'ctx')
- k_grad: bfloat16 [4, 4096, 512], P('dp', 'ctx')
- v_grad: bfloat16 [4, 4096, 512], P('dp', 'ctx')
Inputs may be any that keep to these rules, and one draw needn't show every extreme that they name: `segment_ids`: document numbers never fall along a sequence; each document holds 1 to 2048 tokens and one holds exactly 2048. `loss_mask`: the last token of every sequence counts.
All inputs are finite; a program needn't handle non-finite values.
Results may differ from a plain program's by a relative error of at most 0.024.
Values may be sent and summed in bfloat16 or wider, within the bound.
No kernel may reach another device: no remote copies, remote signals or barrier semaphores. Data moves between devices by JAX's collectives and lax.ppermute only.
A program may use at most 128 MiB of HBM per device.

v0:
```python
import math, functools
import jax, jax.numpy as jnp
from jax import lax
from jax.sharding import PartitionSpec as P
from jax.experimental import pallas as pl
from jax.experimental.pallas import tpu as pltpu

NEG = -1e30
CH = math.log2(math.e) / math.sqrt(128)
BF, F32 = jnp.bfloat16, jnp.float32
NB = 9
NT = (((1,), (1,)), ((), ()))


def mm(a, b):
    return jnp.dot(a, b, preferred_element_type=F32)


def mmt(a, b):
    return lax.dot_general(a, b, NT, preferred_element_type=F32)


def run_heads(score, weigh, output, dscore, dvalue, dkey, dquery, start):
    R = range(NB)

    def pair(i, _):
        S = [start(2 * i), start(2 * i + 1)]
        for t in (0, 1):
            for b in R:
                score(t, S[t], b)
        for t in (0, 1):
            for b in R:
                weigh(t, S[t], b)
        for t in (0, 1):
            output(t, S[t])
        for t in (0, 1):
            for b in R:
                dscore(t, S[t], b)
        for t in (0, 1):
            for b in R:
                dvalue(t, S[t], b)
        for t in (0, 1):
            for b in R:
                dkey(t, S[t], b)
        for t in (0, 1):
            dquery(t, S[t])
        return 0

    lax.fori_loop(0, 4, pair, 0)


def attend_kernel(s_ref, qo_ref, qs_ref, go_ref, gs_ref, own_ref, za_ref, zc_ref, y_ref, tally_ref,
                  oo_ref, dqo_ref, swap_ref, p_ref, loc_ref, kk, vv, kt, vt, bias, sc, pp, ds, dka, dva):
    core, z, y = s_ref[0], s_ref[1], s_ref[2]
    chip = 4 * z + y
    blocks = [(own_ref, (), None), (za_ref, (), chip - 4), (zc_ref, (), chip - 8)]
    for s in (1, 2, 3):
        turned = (y - s) & 3
        blocks.append((y_ref, (turned, 0), 4 * z - 4 + turned))
        blocks.append((y_ref, (turned, 1), chip - s - jnp.where(y >= s, 0, 4)))
    lane = lax.broadcasted_iota(jnp.int32, (1, 128), 1)
    t_seg = jnp.concatenate([own_ref[0, 256:257], own_ref[1, 256:257]], axis=1).astype(F32)
    t_mask = jnp.concatenate([own_ref[0, 257:258], own_ref[1, 257:258]], axis=1).astype(F32)
    t_pos = jnp.concatenate([core * 128 + lane, (1 - core) * 128 + lane], axis=1)
    key = lax.broadcasted_iota(jnp.int32, (128, 256), 0)
    for b, (ref, pre, idx) in enumerate(blocks):
        for o in range(2):
            r0 = b * 256 + o * 128
            k = ref[pre + (o, slice(0, 128))]
            v = ref[pre + (o, slice(128, 256))]
            kk[r0:r0 + 128] = k
            vv[r0:r0 + 128] = v
            kt[:, r0:r0 + 128] = k.T
            vt[:, r0:r0 + 128] = v.T
            k_seg = ref[pre + (o, slice(256, 257))].astype(F32)
            n = [jnp.sum((k_seg < s).astype(F32), axis=1, keepdims=True) for s in (1, 2, 3)]
            first = jnp.where(t_seg == 3, n[2], jnp.where(t_seg == 2, n[1], jnp.where(t_seg == 1, n[0], 0.0)))
            first = first.astype(jnp.int32)
            if idx is None:
                at = core * 128 if o == 0 else (1 - core) * 128
                ok = (key >= first) & (key + at <= t_pos)
            else:
                first = jnp.where(idx >= 0, first, 128)
                ok = key >= first
            bias[r0:r0 + 128] = jnp.where(ok, 0.0, NEG)
    dka[...] = jnp.zeros_like(dka)
    dva[...] = jnp.zeros_like(dva)

    def load(h):
        cols = pl.ds(pl.multiple_of(h * 128, 128), 128)
        q = jnp.concatenate([qo_ref[:, cols], qs_ref[:, cols]], axis=0)
        g = jnp.concatenate([go_ref[:, cols], gs_ref[:, cols]], axis=0)
        return cols, q, g

    def score(t, st, b):
        rows = slice(b * 256, b * 256 + 256)
        s = mmt(kk[rows], st["q"]) + bias[rows]
        sc[t, rows] = s
        top = jnp.max(s.reshape(32, 8, 256), axis=0)
        st["top"] = top if b == 0 else jnp.maximum(st["top"], top)

    def weigh(t, st, b):
        if b == 0:
            st["top"] = jnp.max(st["top"], axis=0, keepdims=True) * CH
        rows = slice(b * 256, b * 256 + 256)
        p = jnp.exp2(sc[t, rows] * CH - st["top"])
        part = jnp.sum(p.reshape(32, 8, 256), axis=0)
        st["mass"] = part if b == 0 else st["mass"] + part
        pp[t, rows] = p.astype(BF)

    def output(t, st):
        inv = 1.0 / jnp.sum(st["mass"], axis=0, keepdims=True)
        ot = (mm(vt[...], pp[t]) * inv).astype(BF)
        out = ot.T
        oo_ref[:, st["cols"]] = out[:128]
        swap_ref[0, :, st["cols"]] = out[128:]
        st["delta"] = jnp.sum(ot.astype(F32) * st["g"].T.astype(F32), axis=0, keepdims=True)
        st["inv"] = inv * t_mask
        col = jnp.broadcast_to(st["inv"], (128, 256)).T
        st["qn"] = (st["q"].astype(F32) * col).astype(BF)
        st["gn"] = (st["g"].astype(F32) * col).astype(BF)

    def dscore(t, st, b):
        rows = slice(b * 256, b * 256 + 256)
        ds[t, rows] = (pp[t, rows].astype(F32) * (mmt(vv[rows], st["g"]) - st["delta"])).astype(BF)

    def dvalue(t, st, b):
        rows = slice(b * 256, b * 256 + 256)
        dva[rows] += mm(pp[t, rows], st["gn"])

    def dkey(t, st, b):
        rows = slice(b * 256, b * 256 + 256)
        dka[rows] += mm(ds[t, rows], st["qn"])

    def dquery(t, st):
        dq = (mm(kt[...], ds[t]) * (st["inv"] * (1.0 / math.sqrt(128)))).astype(BF).T
        dqo_ref[:, st["cols"]] = dq[:128]
        swap_ref[1, :, st["cols"]] = dq[128:]

    def start(h):
        st = {}
        st["cols"], st["q"], st["g"] = load(h)
        return st

    run_heads(score, weigh, output, dscore, dvalue, dkey, dquery, start)
    tally = tally_ref[...]
    high = jnp.floor(tally * (1 / 32))
    digits = jnp.concatenate([high, tally - 32 * high], axis=0).astype(BF)
    for b in range(NB):
        for o in range(2):
            rows = slice(b * 256 + o * 128, b * 256 + o * 128 + 128)
            if b < 3:
                loc_ref[b, o, 0:128] = dka[rows]
                loc_ref[b, o, 128:256] = dva[rows]
            else:
                turned = (y - (b - 1) // 2) & 3
                p_ref[turned, (b - 3) % 2, o, 0:128] = dka[rows].astype(BF)
                p_ref[turned, (b - 3) % 2, o, 128:256] = dva[rows].astype(BF)
                p_ref[turned, (b - 3) % 2, o, 256:272] = digits


def whole(a):
    return pl.BlockSpec(a.shape, lambda i, s, n=len(a.shape): (0,) * n)


def of_head(j):
    return pl.BlockSpec((None, 2, 272, 128), lambda i, s: (j, 0, 0, 0))


def attend(scal, j, q, qs, g, gs, own, za, zc, ys, tally):
    wide = lambda f: pl.BlockSpec((128, 1024), f)
    mine = wide(lambda i, s: (0, s[0] * 2 + j))
    other = wide(lambda i, s: (0, j))
    rows = jax.ShapeDtypeStruct((128, 1024), BF)
    pair = jax.ShapeDtypeStruct((2, 128, 1024), BF)
    loc = jax.ShapeDtypeStruct((3, 2, 256, 128), F32)
    outs = [rows, rows, pair, jax.ShapeDtypeStruct((4, 2, 2, 272, 128), BF), loc]
    n = NB * 256
    ins = (own, za, zc, ys, tally)
    return pl.pallas_call(
        attend_kernel,
        out_shape=outs,
        grid_spec=pltpu.PrefetchScalarGridSpec(
            num_scalar_prefetch=1,
            grid=(1,),
            in_specs=[mine, other, mine, other] + [of_head(j)] * 3 + [whole(ys), whole(tally)],
            out_specs=[whole(o) for o in outs],
            scratch_shapes=[
                pltpu.VMEM((n, 128), BF), pltpu.VMEM((n, 128), BF), pltpu.VMEM((128, n), BF), pltpu.VMEM((128, n), BF),
                pltpu.VMEM((n, 256), F32), pltpu.VMEM((2, n, 256), F32), pltpu.VMEM((2, n, 256), BF),
                pltpu.VMEM((2, n, 256), BF), pltpu.VMEM((n, 128), F32), pltpu.VMEM((n, 128), F32),
            ],
        ),
        compiler_params=pltpu.CompilerParams(vmem_limit_bytes=60 * 2**20),
        cost_estimate=pl.CostEstimate(flops=15 * 2**30, bytes_accessed=4 * 2**20, transcendentals=5 * 2**20),
        name="attend",
    )(scal, q, qs, g, gs, *ins)


def small(kernel, scal, ins, outs, name, head=None):
    return pl.pallas_call(
        kernel,
        out_shape=outs,
        grid_spec=pltpu.PrefetchScalarGridSpec(
            num_scalar_prefetch=1,
            grid=(1,),
            in_specs=[whole(a) if head is None else of_head(head) for a in ins],
            out_specs=[whole(o) for o in outs],
        ),
        compiler_params=pltpu.CompilerParams(vmem_limit_bytes=60 * 2**20),
        name=name,
    )(scal, *ins)


def spread_kernel(s_ref, own_ref, za_ref, zc_ref, out_ref):
    y = s_ref[2]
    for t in range(4):
        out_ref[t, 0] = za_ref[...]

        @pl.when(y < t)
        def _():
            out_ref[t, 1] = own_ref[...]

        @pl.when(y >= t)
        def _():
            out_ref[t, 1] = zc_ref[...]


def sum_kernel(s_ref, got, loc_ref, tally_ref, a_mine, a_theirs, c_mine, c_theirs, here, here_theirs, total):
    y = s_ref[2]
    a, c, h, tally = loc_ref[1], loc_ref[2], loc_ref[0], tally_ref[...]
    for s in (1, 2, 3):
        t = (y + s) & 3
        a = a + got[t, 0, :, 0:256].astype(F32)
        b = got[t, 1, :, 0:256].astype(F32)
        h = h + jnp.where(y + s < 4, b, 0.0)
        c = c + jnp.where(y + s < 4, 0.0, b)
        d = got[t, 0, 0, 256:272].astype(F32)
        tally = tally + 32.0 * d[:8] + d[8:]
    a_mine[...] = a[0].astype(BF)
    a_theirs[...] = a[1].astype(BF)
    c_mine[...] = c[0].astype(BF)
    c_theirs[...] = c[1].astype(BF)
    here[...] = h[0]
    here_theirs[...] = h[1].astype(BF)
    if total is not None:
        total[...] = tally


def sum_both_kernel(s_ref, got, loc_ref, tally_ref, *refs):
    olds, news = refs[:6], refs[6:12]
    for old, new in zip(olds, news):
        new[0] = old[...]
    sum_kernel(s_ref, got, loc_ref, tally_ref, *[new.at[1] for new in news], None)


def final_kernel(s_ref, tally_ref, *refs):
    core = s_ref[0]
    dk_ref, dv_ref = refs[6:]
    scale = (4.0 * 4096) / tally_ref[0:1]
    for j in range(2):
        for c, three in ((core, refs[:3]), (1 - core, refs[3:6])):
            t = sum(r[j].astype(F32) for r in three) * scale
            cols = pl.ds(pl.multiple_of(c * 256 + j * 128, 128), 128)
            dk_ref[:, cols] = (t[0:128] * (1.0 / math.sqrt(128))).astype(BF)
            dv_ref[:, cols] = t[128:256].astype(BF)


def rows_kernel(s_ref, oo0, oo1, dq0, dq1, r0, r1, tally_ref, out_ref, dq_ref):
    core = s_ref[0]
    scale = (4.0 * 4096) / tally_ref[0:1, 0:1]
    for j, (o, d, r) in enumerate(((oo0, dq0, r0), (oo1, dq1, r1))):
        mine = pl.ds(pl.multiple_of(core * 2048 + j * 1024, 128), 1024)
        theirs = pl.ds(pl.multiple_of((1 - core) * 2048 + j * 1024, 128), 1024)
        out_ref[:, mine] = o[...]
        out_ref[:, theirs] = r[0]
        dq_ref[:, mine] = (d[...].astype(F32) * scale).astype(BF)
        dq_ref[:, theirs] = (r[1].astype(F32) * scale).astype(BF)


def shard(queries, keys, values, out_grad, segment_ids, loss_mask):
    me = lax.axis_index("ctx")
    core, y, z = me & 1, (me >> 1) & 3, me >> 3
    q, k, v, g = queries[0], keys[0], values[0], out_grad[0]

    def send(x, target, turn=False):
        pairs = []
        for i in range(32):
            zz, yy, cc = target(i // 8, i // 2 % 4, i % 2)
            if turn or 0 <= zz < 4:
                pairs.append((i, (zz % 4 * 4 + yy % 4) * 2 + cc % 2))
        return lax.ppermute(x, "ctx", pairs)

    swap = lambda x: send(x, lambda z, y, c: (z, y, c + 1))
    along_z = lambda x, a, turn=False: send(x, lambda z, y, c: (z + a, y, c), turn)
    rows_of_y = [[(zz * 4 + yy) * 2 + cc for yy in range(4)] for zz in range(4) for cc in range(2)]
    trade_y = lambda x: lax.all_to_all(x, "ctx", 0, 0, axis_index_groups=rows_of_y)

    info = jnp.concatenate([segment_ids.astype(BF), loss_mask.astype(BF), jnp.zeros((14, 128), BF)], axis=0)

    def payload(c):
        heads = lambda a: lax.dynamic_slice(a, (0, c * 256), (128, 256)).reshape(128, 2, 128).transpose(1, 0, 2)
        return jnp.concatenate([heads(k), heads(v), jnp.broadcast_to(info, (2, 16, 128))], axis=1)

    own = jnp.stack([payload(core), swap(payload(1 - core))], axis=1)
    half = lambda a: lax.dynamic_slice(a, (0, (1 - core) * 2048), (128, 2048))
    qs, gs = swap(half(q)), swap(half(g))
    za, zc = along_z(own, 1, True), along_z(own, 2)
    scal = jnp.stack([core, z, y]).astype(jnp.int32)

    counted = jnp.broadcast_to(jnp.sum(za[0][:, 257].astype(F32)), (8, 128))
    for step in (1, 2):
        counted = counted + lax.ppermute(counted, "dp", [(i, i ^ step) for i in range(4)])

    kind = jax.ShapeDtypeStruct
    four = kind((4, 2, 2, 272, 128), BF)
    ys = [trade_y(small(spread_kernel, scal, (own, za, zc), [four], "spread", head=j)[0]) for j in range(2)]

    side, side32 = kind((256, 128), BF), kind((256, 128), F32)
    sums = [side] * 4 + [side32, side, kind((8, 128), F32)]
    to = lambda x, a, c: send(x, lambda z, yy, cc: (z + a, yy, cc + c))
    oo0, dq0, pair0, part0, loc0 = attend(scal, 0, q, qs, g, gs, own, za, zc, ys[0], counted)
    got0 = trade_y(part0)
    oo1, dq1, pair1, part1, loc1 = attend(scal, 1, q, qs, g, gs, own, za, zc, ys[1], counted)
    first = small(sum_kernel, scal, (got0, loc0, counted), sums, "sum_first")
    tally = first[-1]
    sides, sides32 = kind((2, 256, 128), BF), kind((2, 256, 128), F32)
    a_mine, a_theirs, c_mine, c_theirs, here, here_theirs = small(
        sum_both_kernel, scal, (trade_y(part1), loc1, counted, *first[:-1]), [sides] * 4 + [sides32, sides], "sum_both"
    )
    kv = (here, to(a_mine, -1, 0), to(c_mine, -2, 0), swap(here_theirs), to(a_theirs, -1, 1), to(c_theirs, -2, 1))
    for step in (1, 2):
        tally = tally + send(tally, lambda z, y, c: (z ^ step, y, c))
    wide = kind((128, 4096), BF)
    attn, dq = small(rows_kernel, scal, (oo0, oo1, dq0, dq1, swap(pair0), swap(pair1), tally), [wide] * 2, "rows")
    dk, dv = small(final_kernel, scal, (tally, *kv), [kind((128, 512), BF)] * 2, "final")
    return attn[None], dq[None], dk[None], dv[None]


def solution(mesh):
    rows, ids = P("dp", "ctx", None), P("dp", "ctx")
    return jax.shard_map(
        shard, mesh=mesh, in_specs=(rows,) * 4 + (ids,) * 2, out_specs=(rows,) * 4, check_vma=False
    )
```

profile of v0, /device:TPU:1, one launch (start us, length us, event | category | flops | bytes accessed | tf_op | source)
XLA Modules:
  0.0 138.5 jit_solution(13776615968874476281)
XLA Ops:
  2.9 1.5 %collective-permute-start.2 = (bf16[2,272,128]{2,1,0:T(8,128)(2,1)S(1)}, bf16[2,272,128]{2,1,0:T(8,128)(2,1)S(1)}, u32[]{:S(2)}, u32[]{:S(2)}) collective-permute-start(bf16[2,272,128]{2,1,0:T(8,128)(2,1)S(1)} %get-tuple-element.63), channel_id=1, source_target_pairs={{0,1},{1,0},{2,3},{3,2},{4,5},{5,4},{6,7},{7,6},{8,9},{9,8},{10,11... | collective-permute-start | bytes 417800 | tf_op jit(solution)/shard_map/ppermute | solution.py:292
  5.4 1.8 %collective-permute-start.3 = (bf16[2,2,272,128]{3,2,1,0:T(8,128)(2,1)S(1)}, bf16[2,2,272,128]{3,2,1,0:T(8,128)(2,1)S(1)}, u32[]{:S(2)}, u32[]{:S(2)}) collective-permute-start(bf16[2,2,272,128]{3,2,1,0:T(8,128)(2,1)S(1)} %pad_maximum_fusion.own_ref), channel_id=1, source_target_pairs={{0,8},{1,9},{2,10},{3,11},{4,12},{5,13},{6,14},{7,15},{8,16},{9,17... | collective-permute-start | bytes 835592 | tf_op jit(solution)/shard_map/ppermute | solution.py:292
  7.2 5.2 %collective-permute-start.4 = (bf16[2,2,272,128]{3,2,1,0:T(8,128)(2,1)S(1)}, bf16[2,2,272,128]{3,2,1,0:T(8,128)(2,1)S(1)}, u32[]{:S(2)}, u32[]{:S(2)}) collective-permute-start(bf16[2,2,272,128]{3,2,1,0:T(8,128)(2,1)S(1)} %pad_maximum_fusion.own_ref), channel_id=1, source_target_pairs={{0,16},{1,17},{2,18},{3,19},{4,20},{5,21},{6,22},{7,23},{8,24},{9,... | collective-permute-start | bytes 835592 | tf_op jit(solution)/shard_map/ppermute | solution.py:292
  14.1 2.0 %collective-permute-done.3.za_ref = bf16[2,2,272,128]{3,2,1,0:T(8,128)(2,1)S(1)} collective-permute-done((bf16[2,2,272,128]{3,2,1,0:T(8,128)(2,1)S(1)}, bf16[2,2,272,128]{3,2,1,0:T(8,128)(2,1)S(1)}, u32[]{:S(2)}, u32[]{:S(2)}) %collective-permute-start.3) | collective-permute-done | bytes 278560 | tf_op jit(solution)/shard_map/ppermute | solution.py:292
  16.1 2.9 %collective-permute-done.4.zc_ref = bf16[2,2,272,128]{3,2,1,0:T(8,128)(2,1)S(1)} collective-permute-done((bf16[2,2,272,128]{3,2,1,0:T(8,128)(2,1)S(1)}, bf16[2,2,272,128]{3,2,1,0:T(8,128)(2,1)S(1)}, u32[]{:S(2)}, u32[]{:S(2)}) %collective-permute-start.4) | collective-permute-done | bytes 278560 | tf_op jit(solution)/shard_map/ppermute | solution.py:292
  19.7 2.8 %spread.2 = bf16[4,2,2,272,128]{4,3,2,1,0:T(8,128)(2,1)} custom-call(s32[3]{0:T(128)} %pad_add_fusion.s_ref, bf16[2,2,272,128]{3,2,1,0:T(8,128)(2,1)} %copy-done.2, bf16[2,2,272,128]{3,2,1,0:T(8,128)(2,1)} %copy-done.3, bf16[2,2,272,128]{3,2,1,0:T(8,128)(2,1)} %copy-done.7), custom_call_target="tpu_custom_call" | custom-call | tf_op jit(solution)/shard_map/spread/pallas_call | solution.py:201
  22.5 4.3 %all-to-all-start = ((bf16[4,2,2,272,128]{4,3,2,1,0:T(8,128)(2,1)}), bf16[4,2,2,272,128]{4,3,2,1,0:T(8,128)(2,1)S(1)}, u32[]{:S(2)}, u32[]{:S(2)}) async-start(bf16[4,2,2,272,128]{4,3,2,1,0:T(8,128)(2,1)} %spread.2), calls=%async_computation | async-start | bytes 2228224 | tf_op jit(solution)/shard_map/all_to_all | solution.py:297
  26.9 1.5 %collective-permute-start.1 = (bf16[128,2048]{1,0:T(8,128)(2,1)S(1)}, bf16[128,2048]{1,0:T(8,128)(2,1)}, u32[]{:S(2)}, u32[]{:S(2)}) collective-permute-start(bf16[128,2048]{1,0:T(8,128)(2,1)S(1)} %dynamic-slice_bitcast_fusion), channel_id=1, source_target_pairs={{0,1},{1,0},{2,3},{3,2},{4,5},{5,4},{6,7},{7,6},{8,9},{9,8},{10,11... | collective-permute-start | bytes 1572872 | tf_op jit(solution)/shard_map/ppermute | solution.py:292
  29.6 1.3 collective-permute-start.5
  30.9 1.5 %collective-permute-done.5 = f32[8,128]{1,0:T(8,128)S(1)} collective-permute-done((f32[8,128]{1,0:T(8,128)S(1)}, f32[8,128]{1,0:T(8,128)S(1)}, u32[]{:S(2)}, u32[]{:S(2)}) %collective-permute-start.5) | collective-permute-done | bytes 4128 | tf_op jit(solution)/shard_map/ppermute | solution.py:313
  33.1 2.8 %collective-permute-start.6 = (f32[8,128]{1,0:T(8,128)S(1)}, f32[8,128]{1,0:T(8,128)S(1)}, u32[]{:S(2)}, u32[]{:S(2)}) collective-permute-start(f32[8,128]{1,0:T(8,128)S(1)} %broadcast_add_fusion), channel_id=1, source_target_pairs={{0,64},{32,96},{64,0},{96,32},{1,65},{33,97},{65,1},{97,33},{2,66}... | collective-permute-start | bytes 12296 | tf_op jit(solution)/shard_map/ppermute | solution.py:313
  35.9 2.8 %spread.3 = bf16[4,2,2,272,128]{4,3,2,1,0:T(8,128)(2,1)} custom-call(s32[3]{0:T(128)} %pad_add_fusion.s_ref, bf16[2,2,272,128]{3,2,1,0:T(8,128)(2,1)} %copy-done.2, bf16[2,2,272,128]{3,2,1,0:T(8,128)(2,1)} %copy-done.3, bf16[2,2,272,128]{3,2,1,0:T(8,128)(2,1)} %copy-done.7), custom_call_target="tpu_custom_call" | custom-call | tf_op jit(solution)/shard_map/spread/pallas_call | solution.py:201
  40.0 1.3 all-to-all-done.y_ref
  41.3 3.5 %all-to-all-start.1 = ((bf16[4,2,2,272,128]{4,3,2,1,0:T(8,128)(2,1)}), bf16[4,2,2,272,128]{4,3,2,1,0:T(8,128)(2,1)S(1)}, u32[]{:S(2)}, u32[]{:S(2)}) async-start(bf16[4,2,2,272,128]{4,3,2,1,0:T(8,128)(2,1)} %spread.3), calls=%async_computation.1 | async-start | bytes 2228224 | tf_op jit(solution)/shard_map/all_to_all | solution.py:297
  44.8 21.9 %attend.2 = (bf16[128,1024]{1,0:T(8,128)(2,1)}, bf16[128,1024]{1,0:T(8,128)(2,1)}, bf16[2,128,1024]{2,1,0:T(8,128)(2,1)}, bf16[4,2,2,272,128]{4,3,2,1,0:T(8,128)(2,1)}, f32[3,2,256,128]{3,2,1,0:T(8,128)}) custom-call(s32[3]{0:T(128)} %pad_add_fusion.s_ref, bf16[128,4096]{1,0:T(8,128)(2,1)} %bitcast.34, bf16[128,2048]{1,0:T(8,128)(2,1)} %collective-permute-done.qs_ref, ...), custom_call_target="tpu_custom_call" | custom-call | flops 16106127360 | bytes 4194304 | tf_op jit(solution)/shard_map/attend/pallas_call | solution.py:180
  67.7 4.2 %all-to-all-start.2 = ((bf16[4,2,2,272,128]{4,3,2,1,0:T(8,128)(2,1)}), bf16[4,2,2,272,128]{4,3,2,1,0:T(8,128)(2,1)S(1)}, u32[]{:S(2)}, u32[]{:S(2)}) async-start(bf16[4,2,2,272,128]{4,3,2,1,0:T(8,128)(2,1)} %get-tuple-element.37), calls=%async_computation.2 | async-start | bytes 2228224 | tf_op jit(solution)/shard_map/all_to_all | solution.py:297
  71.9 21.9 %attend.3 = (bf16[128,1024]{1,0:T(8,128)(2,1)}, bf16[128,1024]{1,0:T(8,128)(2,1)}, bf16[2,128,1024]{2,1,0:T(8,128)(2,1)}, bf16[4,2,2,272,128]{4,3,2,1,0:T(8,128)(2,1)}, f32[3,2,256,128]{3,2,1,0:T(8,128)}) custom-call(s32[3]{0:T(128)} %pad_add_fusion.s_ref, bf16[128,4096]{1,0:T(8,128)(2,1)} %bitcast.35, bf16[128,2048]{1,0:T(8,128)(2,1)} %collective-permute-done.qs_ref, ...), custom_call_target="tpu_custom_call" | custom-call | flops 16106127360 | bytes 4194304 | tf_op jit(solution)/shard_map/attend/pallas_call | solution.py:180
  94.8 4.2 %all-to-all-start.3 = ((bf16[4,2,2,272,128]{4,3,2,1,0:T(8,128)(2,1)}), bf16[4,2,2,272,128]{4,3,2,1,0:T(8,128)(2,1)S(1)}, u32[]{:S(2)}, u32[]{:S(2)}) async-start(bf16[4,2,2,272,128]{4,3,2,1,0:T(8,128)(2,1)} %get-tuple-element.42), calls=%async_computation.3 | async-start | bytes 2228224 | tf_op jit(solution)/shard_map/all_to_all | solution.py:297
  99.0 3.4 %collective-permute-start.8 = (bf16[2,128,1024]{2,1,0:T(8,128)(2,1)}, bf16[2,128,1024]{2,1,0:T(8,128)(2,1)S(1)}, u32[]{:S(2)}, u32[]{:S(2)}) collective-permute-start(bf16[2,128,1024]{2,1,0:T(8,128)(2,1)} %get-tuple-element.36), channel_id=1, source_target_pairs={{0,1},{1,0},{2,3},{3,2},{4,5},{5,4},{6,7},{7,6},{8,9},{9,8},{10,11... | collective-permute-start | bytes 1572872 | tf_op jit(solution)/shard_map/ppermute | solution.py:292
  102.5 3.0 %sum_first.1 = (bf16[256,128]{1,0:T(8,128)(2,1)}, bf16[256,128]{1,0:T(8,128)(2,1)}, bf16[256,128]{1,0:T(8,128)(2,1)}, bf16[256,128]{1,0:T(8,128)(2,1)}, f32[256,...) custom-call(s32[3]{0:T(128)} %pad_add_fusion.s_ref, bf16[4,2,2,272,128]{4,3,2,1,0:T(8,128)(2,1)} %copy-done, ...), custom_call_target="tpu_custom_call" | custom-call | tf_op jit(solution)/shard_map/sum_first/pallas_call | solution.py:201
  106.7 1.8 %collective-permute-done.9 = f32[8,128]{1,0:T(8,128)S(1)} collective-permute-done((f32[8,128]{1,0:T(8,128)}, f32[8,128]{1,0:T(8,128)S(1)}, u32[]{:S(2)}, u32[]{:S(2)}) %collective-permute-start.9) | collective-permute-done | bytes 4128 | tf_op jit(solution)/shard_map/ppermute | solution.py:292
  109.2 3.7 %collective-permute-start.10 = (f32[8,128]{1,0:T(8,128)S(1)}, f32[8,128]{1,0:T(8,128)S(1)}, u32[]{:S(2)}, u32[]{:S(2)}) collective-permute-start(f32[8,128]{1,0:T(8,128)S(1)} %add.29), channel_id=1, source_target_pairs={{0,16},{1,17},{2,18},{3,19},{4,20},{5,21},{6,22},{7,23},{8,24},{9,... | collective-permute-start | bytes 12296 | tf_op jit(solution)/shard_map/ppermute | solution.py:292
  113.9 3.2 %sum_both.1 = (bf16[2,256,128]{2,1,0:T(8,128)(2,1)}, bf16[2,256,128]{2,1,0:T(8,128)(2,1)}, bf16[2,256,128]{2,1,0:T(8,128)(2,1)}, bf16[2,256,128]{2,1,0:T(8,128)(...) custom-call(s32[3]{0:T(128)} %pad_add_fusion.s_ref, bf16[4,2,2,272,128]{4,3,2,1,0:T(8,128)(2,1)} %copy-done.1, ...), custom_call_target="tpu_custom_call" | custom-call | tf_op jit(solution)/shard_map/sum_both/pallas_call | solution.py:201
  117.1 1.3 collective-permute-start.11
  118.4 1.3 collective-permute-start.12
  119.7 3.0 %collective-permute-start.13 = (bf16[2,256,128]{2,1,0:T(8,128)(2,1)}, bf16[2,256,128]{2,1,0:T(8,128)(2,1)S(1)}, u32[]{:S(2)}, u32[]{:S(2)}) collective-permute-start(bf16[2,256,128]{2,1,0:T(8,128)(2,1)} %get-tuple-element.53), channel_id=1, source_target_pairs={{0,1},{1,0},{2,3},{3,2},{4,5},{5,4},{6,7},{7,6},{8,9},{9,8},{10,11... | collective-permute-start | bytes 393224 | tf_op jit(solution)/shard_map/ppermute | solution.py:292
  122.7 1.3 collective-permute-start.14
  124.0 1.3 collective-permute-start.15
  125.9 3.6 %rows.1 = (bf16[128,4096]{1,0:T(8,128)(2,1)}, bf16[128,4096]{1,0:T(8,128)(2,1)}) custom-call(s32[3]{0:T(128)} %pad_add_fusion.s_ref, bf16[128,1024]{1,0:T(8,128)(2,1)} %get-tuple-element.31.oo0, bf16[128,1024]{1,0:T(8,128)(2,1)} %get-tuple-element.32.oo1, bf16[128,1024]{1,0:T(8,128)(2,1)} %get-tuple-element.33.dq0, bf16[128,1024]{1,0:T(8,128)(2,1)} %get-tuple-element.34.dq1, ...), custom_call_target="tpu_custom_call" | custom-call | tf_op jit(solution)/shard_map/rows/pallas_call | solution.py:201
  129.6 1.8 %collective-permute-done.14.refs_4_ = bf16[2,256,128]{2,1,0:T(8,128)(2,1)S(1)} collective-permute-done((bf16[2,256,128]{2,1,0:T(8,128)(2,1)}, bf16[2,256,128]{2,1,0:T(8,128)(2,1)S(1)}, u32[]{:S(2)}, u32[]{:S(2)}) %collective-permute-start.14) | collective-permute-done | bytes 131104 | tf_op jit(solution)/shard_map/ppermute | solution.py:292
  131.4 3.8 %collective-permute-done.15.refs_5_ = bf16[2,256,128]{2,1,0:T(8,128)(2,1)S(1)} collective-permute-done((bf16[2,256,128]{2,1,0:T(8,128)(2,1)}, bf16[2,256,128]{2,1,0:T(8,128)(2,1)S(1)}, u32[]{:S(2)}, u32[]{:S(2)}) %collective-permute-start.15) | collective-permute-done | bytes 131104 | tf_op jit(solution)/shard_map/ppermute | solution.py:292
  135.8 2.7 %final.1 = (bf16[128,512]{1,0:T(8,128)(2,1)}, bf16[128,512]{1,0:T(8,128)(2,1)}) custom-call(s32[3]{0:T(128)} %pad_add_fusion.s_ref, f32[8,128]{1,0:T(8,128)} %add.30.tally_ref, f32[2,256,128]{2,1,0:T(8,128)} %get-tuple-element.50.refs_0_, bf16[2,256,128]{2,1,0:T(8,128)(2,1)} %copy-done.12, bf16[2,256,128]{2,1,0:T(8,128)(2,1)} %copy-done.13, ...), custom_call_target="tpu_custom_call" | custom-call | tf_op jit(solution)/shard_map/final/pallas_call | solution.py:201
  (81 shorter events, 14.9 us)
Async XLA Ops:
  1.6 10.8 %copy-start.10 = (bf16[1,128,4096]{2,1,0:T(8,128)(2,1)S(1)}, bf16[1,128,4096]{2,1,0:T(8,128)(2,1)}, u32[]{:S(2)}) copy-start(bf16[1,128,4096]{2,1,0:T(8,128)(2,1)} %param.6) | copy-start | bytes 3145732
  2.9 2.5 %collective-permute-start.2 = (bf16[2,272,128]{2,1,0:T(8,128)(2,1)S(1)}, bf16[2,272,128]{2,1,0:T(8,128)(2,1)S(1)}, u32[]{:S(2)}, u32[]{:S(2)}) collective-permute-start(bf16[2,272,128]{2,1,0:T(8,128)(2,1)S(1)} %get-tuple-element.63), channel_id=1, source_target_pairs={{0,1},{1,0},{2,3},{3,2},{4,5},{5,4},{6,7},{7,6},{8,9},{9,8},{10,11... | collective-permute-start | bytes 417800 | tf_op jit(solution)/shard_map/ppermute | solution.py:292
  5.4 13.6 %copy-start.2 = (bf16[2,2,272,128]{3,2,1,0:T(8,128)(2,1)}, bf16[2,2,272,128]{3,2,1,0:T(8,128)(2,1)S(1)}, u32[]{:S(2)}) copy-start(bf16[2,2,272,128]{3,2,1,0:T(8,128)(2,1)S(1)} %pad_maximum_fusion.own_ref) | copy-start | bytes 835588
  5.4 10.6 %collective-permute-start.3 = (bf16[2,2,272,128]{3,2,1,0:T(8,128)(2,1)S(1)}, bf16[2,2,272,128]{3,2,1,0:T(8,128)(2,1)S(1)}, u32[]{:S(2)}, u32[]{:S(2)}) collective-permute-start(bf16[2,2,272,128]{3,2,1,0:T(8,128)(2,1)S(1)} %pad_maximum_fusion.own_ref), channel_id=1, source_target_pairs={{0,8},{1,9},{2,10},{3,11},{4,12},{5,13},{6,14},{7,15},{8,16},{9,17... | collective-permute-start | bytes 835592 | tf_op jit(solution)/shard_map/ppermute | solution.py:292
  7.2 11.8 %collective-permute-start.4 = (bf16[2,2,272,128]{3,2,1,0:T(8,128)(2,1)S(1)}, bf16[2,2,272,128]{3,2,1,0:T(8,128)(2,1)S(1)}, u32[]{:S(2)}, u32[]{:S(2)}) collective-permute-start(bf16[2,2,272,128]{3,2,1,0:T(8,128)(2,1)S(1)} %pad_maximum_fusion.own_ref), channel_id=1, source_target_pairs={{0,16},{1,17},{2,18},{3,19},{4,20},{5,21},{6,22},{7,23},{8,24},{9,... | collective-permute-start | bytes 835592 | tf_op jit(solution)/shard_map/ppermute | solution.py:292
  12.5 32.3 %collective-permute-start = (bf16[128,2048]{1,0:T(8,128)(2,1)S(1)}, bf16[128,2048]{1,0:T(8,128)(2,1)}, u32[]{:S(2)}, u32[]{:S(2)}) collective-permute-start(bf16[128,2048]{1,0:T(8,128)(2,1)S(1)} %dynamic-slice_bitcast_fusion.1), channel_id=1, source_target_pairs={{0,1},{1,0},{2,3},{3,2},{4,5},{5,4},{6,7},{7,6},{8,9},{9,8},{10,11... | collective-permute-start | bytes 1572872 | tf_op jit(solution)/shard_map/ppermute | solution.py:292
  16.1 2.9 %copy-start.3 = (bf16[2,2,272,128]{3,2,1,0:T(8,128)(2,1)}, bf16[2,2,272,128]{3,2,1,0:T(8,128)(2,1)S(1)}, u32[]{:S(2)}) copy-start(bf16[2,2,272,128]{3,2,1,0:T(8,128)(2,1)S(1)} %collective-permute-done.3.za_ref) | copy-start | bytes 835588
  22.5 4.3 %copy-start.11 = (bf16[1,128,4096]{2,1,0:T(8,128)(2,1)S(1)}, bf16[1,128,4096]{2,1,0:T(8,128)(2,1)}, u32[]{:S(2)}) copy-start(bf16[1,128,4096]{2,1,0:T(8,128)(2,1)} %param.9) | copy-start | bytes 3145732
  22.5 5.8 %copy-start.4 = (bf16[2,2,272,128]{3,2,1,0:T(8,128)(2,1)S(1)}, bf16[2,2,272,128]{3,2,1,0:T(8,128)(2,1)}, u32[]{:S(2)}) copy-start(bf16[2,2,272,128]{3,2,1,0:T(8,128)(2,1)} %copy-done.3) | copy-start | bytes 835588
  22.5 18.7 %all-to-all-start = ((bf16[4,2,2,272,128]{4,3,2,1,0:T(8,128)(2,1)}), bf16[4,2,2,272,128]{4,3,2,1,0:T(8,128)(2,1)S(1)}, u32[]{:S(2)}, u32[]{:S(2)}) async-start(bf16[4,2,2,272,128]{4,3,2,1,0:T(8,128)(2,1)} %spread.2), calls=%async_computation | async-start | bytes 2228224 | tf_op jit(solution)/shard_map/all_to_all | solution.py:297
  26.9 17.9 %collective-permute-start.1 = (bf16[128,2048]{1,0:T(8,128)(2,1)S(1)}, bf16[128,2048]{1,0:T(8,128)(2,1)}, u32[]{:S(2)}, u32[]{:S(2)}) collective-permute-start(bf16[128,2048]{1,0:T(8,128)(2,1)S(1)} %dynamic-slice_bitcast_fusion), channel_id=1, source_target_pairs={{0,1},{1,0},{2,3},{3,2},{4,5},{5,4},{6,7},{7,6},{8,9},{9,8},{10,11... | collective-permute-start | bytes 1572872 | tf_op jit(solution)/shard_map/ppermute | solution.py:292
  29.6 2.8 %collective-permute-start.5 = (f32[8,128]{1,0:T(8,128)S(1)}, f32[8,128]{1,0:T(8,128)S(1)}, u32[]{:S(2)}, u32[]{:S(2)}) collective-permute-start(f32[8,128]{1,0:T(8,128)S(1)} %broadcast_in_dim.24), channel_id=1, source_target_pairs={{0,32},{32,0},{64,96},{96,64},{1,33},{33,1},{65,97},{97,65},{2,34}... | collective-permute-start | bytes 12296 | tf_op jit(solution)/shard_map/ppermute | solution.py:313
  33.1 5.6 %collective-permute-start.6 = (f32[8,128]{1,0:T(8,128)S(1)}, f32[8,128]{1,0:T(8,128)S(1)}, u32[]{:S(2)}, u32[]{:S(2)}) collective-permute-start(f32[8,128]{1,0:T(8,128)S(1)} %broadcast_add_fusion), channel_id=1, source_target_pairs={{0,64},{32,96},{64,0},{96,32},{1,65},{33,97},{65,1},{97,33},{2,66}... | collective-permute-start | bytes 12296 | tf_op jit(solution)/shard_map/ppermute | solution.py:313
  41.2 3.6 %copy-start.5 = (bf16[4,2,2,272,128]{4,3,2,1,0:T(8,128)(2,1)}, bf16[4,2,2,272,128]{4,3,2,1,0:T(8,128)(2,1)S(1)}, u32[]{:S(2)}) copy-start(bf16[4,2,2,272,128]{4,3,2,1,0:T(8,128)(2,1)S(1)} %all-to-all-done.y_ref) | copy-start | bytes 3342340
  41.3 25.5 %all-to-all-start.1 = ((bf16[4,2,2,272,128]{4,3,2,1,0:T(8,128)(2,1)}), bf16[4,2,2,272,128]{4,3,2,1,0:T(8,128)(2,1)S(1)}, u32[]{:S(2)}, u32[]{:S(2)}) async-start(bf16[4,2,2,272,128]{4,3,2,1,0:T(8,128)(2,1)} %spread.3), calls=%async_computation.1 | async-start | bytes 2228224 | tf_op jit(solution)/shard_map/all_to_all | solution.py:297
  67.7 26.1 %all-to-all-start.2 = ((bf16[4,2,2,272,128]{4,3,2,1,0:T(8,128)(2,1)}), bf16[4,2,2,272,128]{4,3,2,1,0:T(8,128)(2,1)S(1)}, u32[]{:S(2)}, u32[]{:S(2)}) async-start(bf16[4,2,2,272,128]{4,3,2,1,0:T(8,128)(2,1)} %get-tuple-element.37), calls=%async_computation.2 | async-start | bytes 2228224 | tf_op jit(solution)/shard_map/all_to_all | solution.py:297
  94.8 18.1 %all-to-all-start.3 = ((bf16[4,2,2,272,128]{4,3,2,1,0:T(8,128)(2,1)}), bf16[4,2,2,272,128]{4,3,2,1,0:T(8,128)(2,1)S(1)}, u32[]{:S(2)}, u32[]{:S(2)}) async-start(bf16[4,2,2,272,128]{4,3,2,1,0:T(8,128)(2,1)} %get-tuple-element.42), calls=%async_computation.3 | async-start | bytes 2228224 | tf_op jit(solution)/shard_map/all_to_all | solution.py:297
  99.0 20.6 %collective-permute-start.8 = (bf16[2,128,1024]{2,1,0:T(8,128)(2,1)}, bf16[2,128,1024]{2,1,0:T(8,128)(2,1)S(1)}, u32[]{:S(2)}, u32[]{:S(2)}) collective-permute-start(bf16[2,128,1024]{2,1,0:T(8,128)(2,1)} %get-tuple-element.36), channel_id=1, source_target_pairs={{0,1},{1,0},{2,3},{3,2},{4,5},{5,4},{6,7},{7,6},{8,9},{9,8},{10,11... | collective-permute-start | bytes 1572872 | tf_op jit(solution)/shard_map/ppermute | solution.py:292
  102.5 20.2 %collective-permute-start.7 = (bf16[2,128,1024]{2,1,0:T(8,128)(2,1)}, bf16[2,128,1024]{2,1,0:T(8,128)(2,1)S(1)}, u32[]{:S(2)}, u32[]{:S(2)}) collective-permute-start(bf16[2,128,1024]{2,1,0:T(8,128)(2,1)} %get-tuple-element.35), channel_id=1, source_target_pairs={{0,1},{1,0},{2,3},{3,2},{4,5},{5,4},{6,7},{7,6},{8,9},{9,8},{10,11... | collective-permute-start | bytes 1572872 | tf_op jit(solution)/shard_map/ppermute | solution.py:292
  105.5 3.0 %collective-permute-start.9 = (f32[8,128]{1,0:T(8,128)}, f32[8,128]{1,0:T(8,128)S(1)}, u32[]{:S(2)}, u32[]{:S(2)}) collective-permute-start(f32[8,128]{1,0:T(8,128)} %get-tuple-element.39), channel_id=1, source_target_pairs={{0,8},{1,9},{2,10},{3,11},{4,12},{5,13},{6,14},{7,15},{8,0},{9,1},... | collective-permute-start | bytes 12296 | tf_op jit(solution)/shard_map/ppermute | solution.py:292
  109.2 14.8 %collective-permute-start.10 = (f32[8,128]{1,0:T(8,128)S(1)}, f32[8,128]{1,0:T(8,128)S(1)}, u32[]{:S(2)}, u32[]{:S(2)}) collective-permute-start(f32[8,128]{1,0:T(8,128)S(1)} %add.29), channel_id=1, source_target_pairs={{0,16},{1,17},{2,18},{3,19},{4,20},{5,21},{6,22},{7,23},{8,24},{9,... | collective-permute-start | bytes 12296 | tf_op jit(solution)/shard_map/ppermute | solution.py:292
  117.1 12.4 %collective-permute-start.11 = (bf16[2,256,128]{2,1,0:T(8,128)(2,1)}, bf16[2,256,128]{2,1,0:T(8,128)(2,1)S(1)}, u32[]{:S(2)}, u32[]{:S(2)}) collective-permute-start(bf16[2,256,128]{2,1,0:T(8,128)(2,1)} %get-tuple-element.51), channel_id=1, source_target_pairs={{8,0},{9,1},{10,2},{11,3},{12,4},{13,5},{14,6},{15,7},{16,8},{17,9... | collective-permute-start | bytes 393224 | tf_op jit(solution)/shard_map/ppermute | solution.py:292
  118.4 11.1 %collective-permute-start.12 = (bf16[2,256,128]{2,1,0:T(8,128)(2,1)}, bf16[2,256,128]{2,1,0:T(8,128)(2,1)S(1)}, u32[]{:S(2)}, u32[]{:S(2)}) collective-permute-start(bf16[2,256,128]{2,1,0:T(8,128)(2,1)} %get-tuple-element.52), channel_id=1, source_target_pairs={{16,0},{17,1},{18,2},{19,3},{20,4},{21,5},{22,6},{23,7},{24,8},{25... | collective-permute-start | bytes 393224 | tf_op jit(solution)/shard_map/ppermute | solution.py:292
  119.7 6.2 %copy-start.8 = (bf16[2,128,1024]{2,1,0:T(8,128)(2,1)}, bf16[2,128,1024]{2,1,0:T(8,128)(2,1)S(1)}, u32[]{:S(2)}) copy-start(bf16[2,128,1024]{2,1,0:T(8,128)(2,1)S(1)} %collective-permute-done.8.r1) | copy-start | bytes 1572868
  119.7 9.8 %collective-permute-start.13 = (bf16[2,256,128]{2,1,0:T(8,128)(2,1)}, bf16[2,256,128]{2,1,0:T(8,128)(2,1)S(1)}, u32[]{:S(2)}, u32[]{:S(2)}) collective-permute-start(bf16[2,256,128]{2,1,0:T(8,128)(2,1)} %get-tuple-element.53), channel_id=1, source_target_pairs={{0,1},{1,0},{2,3},{3,2},{4,5},{5,4},{6,7},{7,6},{8,9},{9,8},{10,11... | collective-permute-start | bytes 393224 | tf_op jit(solution)/shard_map/ppermute | solution.py:292
  122.7 3.2 %copy-start.9 = (bf16[2,128,1024]{2,1,0:T(8,128)(2,1)}, bf16[2,128,1024]{2,1,0:T(8,128)(2,1)S(1)}, u32[]{:S(2)}) copy-start(bf16[2,128,1024]{2,1,0:T(8,128)(2,1)S(1)} %collective-permute-done.7.r0) | copy-start | bytes 1572868
  122.7 8.6 %collective-permute-start.14 = (bf16[2,256,128]{2,1,0:T(8,128)(2,1)}, bf16[2,256,128]{2,1,0:T(8,128)(2,1)S(1)}, u32[]{:S(2)}, u32[]{:S(2)}) collective-permute-start(bf16[2,256,128]{2,1,0:T(8,128)(2,1)} %get-tuple-element.54), channel_id=1, source_target_pairs={{8,1},{9,0},{10,3},{11,2},{12,5},{13,4},{14,7},{15,6},{16,9},{17,8... | collective-permute-start | bytes 393224 | tf_op jit(solution)/shard_map/ppermute | solution.py:292
  124.0 11.2 %collective-permute-start.15 = (bf16[2,256,128]{2,1,0:T(8,128)(2,1)}, bf16[2,256,128]{2,1,0:T(8,128)(2,1)S(1)}, u32[]{:S(2)}, u32[]{:S(2)}) collective-permute-start(bf16[2,256,128]{2,1,0:T(8,128)(2,1)} %get-tuple-element.55), channel_id=1, source_target_pairs={{16,1},{17,0},{18,3},{19,2},{20,5},{21,4},{22,7},{23,6},{24,9},{25... | collective-permute-start | bytes 393224 | tf_op jit(solution)/shard_map/ppermute | solution.py:292
  129.5 5.6 %copy-start.12 = (bf16[2,256,128]{2,1,0:T(8,128)(2,1)}, bf16[2,256,128]{2,1,0:T(8,128)(2,1)S(1)}, u32[]{:S(2)}) copy-start(bf16[2,256,128]{2,1,0:T(8,128)(2,1)S(1)} %collective-permute-done.11.refs_1_) | copy-start | bytes 393220
  129.5 5.6 %copy-start.13 = (bf16[2,256,128]{2,1,0:T(8,128)(2,1)}, bf16[2,256,128]{2,1,0:T(8,128)(2,1)S(1)}, u32[]{:S(2)}) copy-start(bf16[2,256,128]{2,1,0:T(8,128)(2,1)S(1)} %collective-permute-done.12.refs_2_) | copy-start | bytes 393220
  129.6 5.6 %copy-start.14 = (bf16[2,256,128]{2,1,0:T(8,128)(2,1)}, bf16[2,256,128]{2,1,0:T(8,128)(2,1)S(1)}, u32[]{:S(2)}) copy-start(bf16[2,256,128]{2,1,0:T(8,128)(2,1)S(1)} %collective-permute-done.13.refs_3_) | copy-start | bytes 393220
  131.4 3.8 %copy-start.15 = (bf16[2,256,128]{2,1,0:T(8,128)(2,1)}, bf16[2,256,128]{2,1,0:T(8,128)(2,1)S(1)}, u32[]{:S(2)}) copy-start(bf16[2,256,128]{2,1,0:T(8,128)(2,1)S(1)} %collective-permute-done.14.refs_4_) | copy-start | bytes 393220
  (7 other events, 8.4 us)
where the time goes:
time: 139 us; the launch traced here: 138 us
  Pallas kernels  61.9 us (45%)
  starting transfers between devices  47.8 us (34%)
  waiting for transfers between devices  16.1 us (12%)
  local copies, waits for them, and re-layouts  7.17 us (5%)
  other arithmetic  4.47 us (3%)
    pallas_call x2, Pallas kernels, attend(): pl.pallas_call(attend_kernel, out_shape=outs, grid_spec=pltpu.PrefetchSca...  43.8 us
    ppermute x14, starting transfers between devices, send(): return lax.ppermute(x, 'ctx', pairs)  27.5 us
    pallas_call x6, Pallas kernels, small(): pl.pallas_call(kernel, out_shape=outs, grid_spec=pltpu.PrefetchScalarGrid...  18.1 us
    all_to_all x4, starting transfers between devices, shard(): lax.all_to_all(x, 'ctx', 0, 0, axis_index_groups=rows_of_y)  16.2 us
    ppermute x14, waiting for transfers between devices, send(): return lax.ppermute(x, 'ctx', pairs)  13.3 us
    unnamed x42, local copies, waits for them, and re-layouts  4.89 us
    ppermute x2, starting transfers between devices, shard(): lax.ppermute(counted, 'dp', [(i, i ^ step) for i in range(4)])  4.11 us
  transfers between devices with their start and end apart: 20, of which 8 were waited for; matrix products, arithmetic and copies ran while one was open for 4% of the time, Pallas kernels for 43%

commit v1 on v0

--- a/solution.py
+++ b/solution.py
@@ -50,7 +50,7 @@
 
 
 def attend_kernel(s_ref, qo_ref, qs_ref, go_ref, gs_ref, own_ref, za_ref, zc_ref, y_ref, tally_ref,
-                  oo_ref, dqo_ref, swap_ref, p_ref, loc_ref, kk, vv, kt, vt, bias, sc, pp, ds, dka, dva):
+                  oo_ref, dqo_ref, swap_ref, p_ref, loc_ref, cnt_ref, kk, vv, kt, vt, bias, sc, pp, ds, dka, dva):
     core, z, y = s_ref[0], s_ref[1], s_ref[2]
     chip = 4 * z + y
     blocks = [(own_ref, (), None), (za_ref, (), chip - 4), (zc_ref, (), chip - 8)]
@@ -144,8 +144,10 @@
 
     run_heads(score, weigh, output, dscore, dvalue, dkey, dquery, start)
     tally = tally_ref[...]
-    high = jnp.floor(tally * (1 / 32))
-    digits = jnp.concatenate([high, tally - 32 * high], axis=0).astype(BF)
+    for s in (1, 2, 3):
+        digits = y_ref[(y - s) & 3, 0, 0, 256:272].astype(F32)
+        tally = tally + 32.0 * digits[2:3] + digits[3:4]
+    cnt_ref[...] = tally
     for b in range(NB):
         for o in range(2):
             rows = slice(b * 256 + o * 128, b * 256 + o * 128 + 128)
@@ -156,7 +158,6 @@
                 turned = (y - (b - 1) // 2) & 3
                 p_ref[turned, (b - 3) % 2, o, 0:128] = dka[rows].astype(BF)
                 p_ref[turned, (b - 3) % 2, o, 128:256] = dva[rows].astype(BF)
-                p_ref[turned, (b - 3) % 2, o, 256:272] = digits
 
 
 def whole(a):
@@ -174,7 +175,7 @@
     rows = jax.ShapeDtypeStruct((128, 1024), BF)
     pair = jax.ShapeDtypeStruct((2, 128, 1024), BF)
     loc = jax.ShapeDtypeStruct((3, 2, 256, 128), F32)
-    outs = [rows, rows, pair, jax.ShapeDtypeStruct((4, 2, 2, 272, 128), BF), loc]
+    outs = [rows, rows, pair, jax.ShapeDtypeStruct((4, 2, 2, 256, 128), BF), loc, jax.ShapeDtypeStruct((8, 128), F32)]
     n = NB * 256
     ins = (own, za, zc, ys, tally)
     return pl.pallas_call(
@@ -204,18 +205,24 @@
         grid_spec=pltpu.PrefetchScalarGridSpec(
             num_scalar_prefetch=1,
             grid=(1,),
-            in_specs=[whole(a) if head is None else of_head(head) for a in ins],
+            in_specs=[of_head(head) if len(a.shape) == 4 and head is not None else whole(a) for a in ins],
             out_specs=[whole(o) for o in outs],
         ),
-        compiler_params=pltpu.CompilerParams(vmem_limit_bytes=60 * 2**20),
+        compiler_params=pltpu.CompilerParams(vmem_limit_bytes=16 * 2**20),
         name=name,
     )(scal, *ins)
 
 
-def spread_kernel(s_ref, own_ref, za_ref, zc_ref, out_ref):
+def spread_kernel(s_ref, own_ref, za_ref, zc_ref, tally_ref, out_ref):
     y = s_ref[2]
+    tally = tally_ref[...]
+    high = jnp.floor(tally * (1 / 32))
+    row = lax.broadcasted_iota(jnp.int32, (16, 128), 0)
+    info = za_ref[0, 256:272].astype(F32)
+    info = jnp.where(row == 2, high[:1], jnp.where(row == 3, (tally - 32 * high)[:1], info)).astype(BF)
     for t in range(4):
         out_ref[t, 0] = za_ref[...]
+        out_ref[t, 0, 0, 256:272] = info
 
         @pl.when(y < t)
         def _():
@@ -226,32 +233,22 @@
             out_ref[t, 1] = zc_ref[...]
 
 
-def sum_kernel(s_ref, got, loc_ref, tally_ref, a_mine, a_theirs, c_mine, c_theirs, here, here_theirs, total):
+def sum_kernel(s_ref, got0, loc0, got1, loc1, a_mine, a_theirs, c_mine, c_theirs, here, here_theirs):
     y = s_ref[2]
-    a, c, h, tally = loc_ref[1], loc_ref[2], loc_ref[0], tally_ref[...]
-    for s in (1, 2, 3):
-        t = (y + s) & 3
-        a = a + got[t, 0, :, 0:256].astype(F32)
-        b = got[t, 1, :, 0:256].astype(F32)
-        h = h + jnp.where(y + s < 4, b, 0.0)
-        c = c + jnp.where(y + s < 4, 0.0, b)
-        d = got[t, 0, 0, 256:272].astype(F32)
-        tally = tally + 32.0 * d[:8] + d[8:]
-    a_mine[...] = a[0].astype(BF)
-    a_theirs[...] = a[1].astype(BF)
-    c_mine[...] = c[0].astype(BF)
-    c_theirs[...] = c[1].astype(BF)
-    here[...] = h[0]
-    here_theirs[...] = h[1].astype(BF)
-    if total is not None:
-        total[...] = tally
-
-
-def sum_both_kernel(s_ref, got, loc_ref, tally_ref, *refs):
-    olds, news = refs[:6], refs[6:12]
-    for old, new in zip(olds, news):
-        new[0] = old[...]
-    sum_kernel(s_ref, got, loc_ref, tally_ref, *[new.at[1] for new in news], None)
+    for j, (got, loc_ref) in enumerate(((got0, loc0), (got1, loc1))):
+        a, c, h = loc_ref[1], loc_ref[2], loc_ref[0]
+        for s in (1, 2, 3):
+            t = (y + s) & 3
+            a = a + got[t, 0].astype(F32)
+            b = got[t, 1].astype(F32)
+            h = h + jnp.where(y + s < 4, b, 0.0)
+            c = c + jnp.where(y + s < 4, 0.0, b)
+        a_mine[j] = a[0].astype(BF)
+        a_theirs[j] = a[1].astype(BF)
+        c_mine[j] = c[0].astype(BF)
+        c_theirs[j] = c[1].astype(BF)
+        here[j] = h[0]
+        here_theirs[j] = h[1].astype(BF)
 
 
 def final_kernel(s_ref, tally_ref, *refs):
@@ -314,19 +311,18 @@
 
     kind = jax.ShapeDtypeStruct
     four = kind((4, 2, 2, 272, 128), BF)
-    ys = [trade_y(small(spread_kernel, scal, (own, za, zc), [four], "spread", head=j)[0]) for j in range(2)]
-
-    side, side32 = kind((256, 128), BF), kind((256, 128), F32)
-    sums = [side] * 4 + [side32, side, kind((8, 128), F32)]
+    ys = [
+        trade_y(small(spread_kernel, scal, (own, za, zc, n), [four], "spread", head=j)[0])
+        for j, n in enumerate((jnp.zeros((8, 128), F32), counted))
+    ]
+
     to = lambda x, a, c: send(x, lambda z, yy, cc: (z + a, yy, cc + c))
-    oo0, dq0, pair0, part0, loc0 = attend(scal, 0, q, qs, g, gs, own, za, zc, ys[0], counted)
+    oo0, dq0, pair0, part0, loc0, _ = attend(scal, 0, q, qs, g, gs, own, za, zc, ys[0], counted)
     got0 = trade_y(part0)
-    oo1, dq1, pair1, part1, loc1 = attend(scal, 1, q, qs, g, gs, own, za, zc, ys[1], counted)
-    first = small(sum_kernel, scal, (got0, loc0, counted), sums, "sum_first")
-    tally = first[-1]
+    oo1, dq1, pair1, part1, loc1, tally = attend(scal, 1, q, qs, g, gs, own, za, zc, ys[1], counted)
     sides, sides32 = kind((2, 256, 128), BF), kind((2, 256, 128), F32)
     a_mine, a_theirs, c_mine, c_theirs, here, here_theirs = small(
-        sum_both_kernel, scal, (trade_y(part1), loc1, counted, *first[:-1]), [sides] * 4 + [sides32, sides], "sum_both"
+        sum_kernel, scal, (got0, loc0, trade_y(part1), loc1), [sides] * 4 + [sides32, sides], "sum"
     )
     kv = (here, to(a_mine, -1, 0), to(c_mine, -2, 0), swap(here_theirs), to(a_theirs, -1, 1), to(c_theirs, -2, 1))
     for step in (1, 2):

time: 139 us -> 133 us (0.957)
  Pallas kernels: 61.9 us -> 52.5 us
  starting transfers between devices: 47.8 us -> 50.2 us
  waiting for transfers between devices: 16.1 us -> 17.9 us
    pallas_call x6 -> x5, Pallas kernels: 18.1 us -> 8.74 us  [small(): pl.pallas_call(kernel, out_shape=outs, grid_spec=pltpu.PrefetchScalarGrid...]
    unnamed x42 -> x38, local copies, waits for them, and re-layouts: 4.89 us -> 2.66 us
    ppermute x14, starting transfers between devices: 27.5 us -> 29.7 us  [send(): return lax.ppermute(x, 'ctx', pairs)]
    dynamic_slice x2, local copies, waits for them, and re-layouts: 0.08 us -> 1.69 us  [shard(): half = lambda a: lax.dynamic_slice(a, (0, (1 - core) * 2048), (128, 2048))]
  transfers between devices with their start and end apart: 20 -> 20, of which waited for: 8 -> 10; matrix products, arithmetic and copies ran while one was open for 4% -> 3% of each run, Pallas kernels for 43% -> 39%
where the time goes in v1:
time: 133 us; the launch traced here: 132 us
  Pallas kernels  52.5 us (39%)
  starting transfers between devices  50.2 us (38%)
  waiting for transfers between devices  17.9 us (13%)
  local copies, waits for them, and re-layouts  6.54 us (5%)
  other arithmetic  3.42 us (3%)
    pallas_call x2, Pallas kernels, attend(): pl.pallas_call(attend_kernel, out_shape=outs, grid_spec=pltpu.PrefetchSca...  43.8 us
    ppermute x14, starting transfers between devices, send(): return lax.ppermute(x, 'ctx', pairs)  29.7 us
    all_to_all x4, starting transfers between devices, shard(): lax.all_to_all(x, 'ctx', 0, 0, axis_index_groups=rows_of_y)  16.4 us
    ppermute x14, waiting for transfers between devices, send(): return lax.ppermute(x, 'ctx', pairs)  12.7 us
    pallas_call x5, Pallas kernels, small(): pl.pallas_call(kernel, out_shape=outs, grid_spec=pltpu.PrefetchScalarGrid...  8.74 us
    ppermute x2, starting transfers between devices, shard(): lax.ppermute(counted, 'dp', [(i, i ^ step) for i in range(4)])  4.11 us
    ppermute x2, waiting for transfers between devices, shard(): lax.ppermute(counted, 'dp', [(i, i ^ step) for i in range(4)])  2.76 us
    unnamed x38, local copies, waits for them, and re-layouts  2.66 us
  transfers between devices with their start and end apart: 20, of which 10 were waited for; matrix products, arithmetic and copies ran while one was open for 3% of the time, Pallas kernels for 39%

profile of v1, /device:TPU:1, one launch (start us, length us, event | category | flops | bytes accessed | tf_op | source)
XLA Modules:
  0.0 131.6 jit_solution(14856096180781062217)
XLA Ops:
  4.1 1.5 %collective-permute-start.2 = (bf16[2,272,128]{2,1,0:T(8,128)(2,1)S(1)}, bf16[2,272,128]{2,1,0:T(8,128)(2,1)S(1)}, u32[]{:S(2)}, u32[]{:S(2)}) collective-permute-start(bf16[2,272,128]{2,1,0:T(8,128)(2,1)S(1)} %get-tuple-element.51), channel_id=1, source_target_pairs={{0,1},{1,0},{2,3},{3,2},{4,5},{5,4},{6,7},{7,6},{8,9},{9,8},{10,11... | collective-permute-start | bytes 417800 | tf_op jit(solution)/shard_map/ppermute | solution.py:289
  6.7 1.8 %collective-permute-start.3 = (bf16[2,2,272,128]{3,2,1,0:T(8,128)(2,1)S(1)}, bf16[2,2,272,128]{3,2,1,0:T(8,128)(2,1)S(1)}, u32[]{:S(2)}, u32[]{:S(2)}) collective-permute-start(bf16[2,2,272,128]{3,2,1,0:T(8,128)(2,1)S(1)} %pad_maximum_fusion.own_ref), channel_id=1, source_target_pairs={{0,8},{1,9},{2,10},{3,11},{4,12},{5,13},{6,14},{7,15},{8,16},{9,17... | collective-permute-start | bytes 835592 | tf_op jit(solution)/shard_map/ppermute | solution.py:289
  8.5 5.2 %collective-permute-start.4 = (bf16[2,2,272,128]{3,2,1,0:T(8,128)(2,1)S(1)}, bf16[2,2,272,128]{3,2,1,0:T(8,128)(2,1)S(1)}, u32[]{:S(2)}, u32[]{:S(2)}) collective-permute-start(bf16[2,2,272,128]{3,2,1,0:T(8,128)(2,1)S(1)} %pad_maximum_fusion.own_ref), channel_id=1, source_target_pairs={{0,16},{1,17},{2,18},{3,19},{4,20},{5,21},{6,22},{7,23},{8,24},{9,... | collective-permute-start | bytes 835592 | tf_op jit(solution)/shard_map/ppermute | solution.py:289
  15.5 1.8 %collective-permute-done.3.za_ref = bf16[2,2,272,128]{3,2,1,0:T(8,128)(2,1)S(1)} collective-permute-done((bf16[2,2,272,128]{3,2,1,0:T(8,128)(2,1)S(1)}, bf16[2,2,272,128]{3,2,1,0:T(8,128)(2,1)S(1)}, u32[]{:S(2)}, u32[]{:S(2)}) %collective-permute-start.3) | collective-permute-done | bytes 278560 | tf_op jit(solution)/shard_map/ppermute | solution.py:289
  17.3 2.9 %collective-permute-done.4.zc_ref = bf16[2,2,272,128]{3,2,1,0:T(8,128)(2,1)S(1)} collective-permute-done((bf16[2,2,272,128]{3,2,1,0:T(8,128)(2,1)S(1)}, bf16[2,2,272,128]{3,2,1,0:T(8,128)(2,1)S(1)}, u32[]{:S(2)}, u32[]{:S(2)}) %collective-permute-start.4) | collective-permute-done | bytes 278560 | tf_op jit(solution)/shard_map/ppermute | solution.py:289
  20.2 1.7 %spread.2 = bf16[4,2,2,272,128]{4,3,2,1,0:T(8,128)(2,1)} custom-call(s32[3]{0:T(128)S(1)} %pad_add_fusion.s_ref, bf16[2,2,272,128]{3,2,1,0:T(8,128)(2,1)S(1)} %pad_maximum_fusion.own_ref, bf16[2,2,272,128]{3,2,1,0:T(8,128)(2,1)S(1)} %collective-permute-done.3.za_ref, bf16[2,2,272,128]{3,2,1,0:T(8,128)(2,1)S(1)} %collective-permute-done.4.zc_ref, ...), custom_call_target="tpu_custom_call" | custom-call | tf_op jit(solution)/shard_map/spread/pallas_call | solution.py:202
  21.9 4.3 %all-to-all-start = ((bf16[4,2,2,272,128]{4,3,2,1,0:T(8,128)(2,1)}), bf16[4,2,2,272,128]{4,3,2,1,0:T(8,128)(2,1)S(1)}, u32[]{:S(2)}, u32[]{:S(2)}) async-start(bf16[4,2,2,272,128]{4,3,2,1,0:T(8,128)(2,1)} %spread.2), calls=%async_computation | async-start | bytes 2228224 | tf_op jit(solution)/shard_map/all_to_all | solution.py:294
  27.0 1.4 %collective-permute-start.1 = (bf16[128,2048]{1,0:T(8,128)(2,1)}, bf16[128,2048]{1,0:T(8,128)(2,1)}, u32[]{:S(2)}, u32[]{:S(2)}) collective-permute-start(bf16[128,2048]{1,0:T(8,128)(2,1)} %dynamic-slice_bitcast_fusion), channel_id=1, source_target_pairs={{0,1},{1,0},{2,3},{3,2},{4,5},{5,4},{6,7},{7,6},{8,9},{9,8},{10,11... | collective-permute-start | bytes 1572872 | tf_op jit(solution)/shard_map/ppermute | solution.py:289
  29.7 1.3 collective-permute-start.5
  31.0 1.5 %collective-permute-done.5 = f32[8,128]{1,0:T(8,128)S(1)} collective-permute-done((f32[8,128]{1,0:T(8,128)S(1)}, f32[8,128]{1,0:T(8,128)S(1)}, u32[]{:S(2)}, u32[]{:S(2)}) %collective-permute-start.5) | collective-permute-done | bytes 4128 | tf_op jit(solution)/shard_map/ppermute | solution.py:310
  33.2 2.8 %collective-permute-start.6 = (f32[8,128]{1,0:T(8,128)S(1)}, f32[8,128]{1,0:T(8,128)S(1)}, u32[]{:S(2)}, u32[]{:S(2)}) collective-permute-start(f32[8,128]{1,0:T(8,128)S(1)} %broadcast_add_fusion), channel_id=1, source_target_pairs={{0,64},{32,96},{64,0},{96,32},{1,65},{33,97},{65,1},{97,33},{2,66}... | collective-permute-start | bytes 12296 | tf_op jit(solution)/shard_map/ppermute | solution.py:310
  36.0 1.2 collective-permute-done.6
  37.9 1.6 %spread.3 = bf16[4,2,2,272,128]{4,3,2,1,0:T(8,128)(2,1)} custom-call(s32[3]{0:T(128)S(1)} %pad_add_fusion.s_ref, bf16[2,2,272,128]{3,2,1,0:T(8,128)(2,1)S(1)} %pad_maximum_fusion.own_ref, bf16[2,2,272,128]{3,2,1,0:T(8,128)(2,1)S(1)} %collective-permute-done.3.za_ref, bf16[2,2,272,128]{3,2,1,0:T(8,128)(2,1)S(1)} %collective-permute-done.4.zc_ref, ...), custom_call_target="tpu_custom_call" | custom-call | tf_op jit(solution)/shard_map/spread/pallas_call | solution.py:202
  40.6 3.5 %all-to-all-start.1 = ((bf16[4,2,2,272,128]{4,3,2,1,0:T(8,128)(2,1)}), bf16[4,2,2,272,128]{4,3,2,1,0:T(8,128)(2,1)S(1)}, u32[]{:S(2)}, u32[]{:S(2)}) async-start(bf16[4,2,2,272,128]{4,3,2,1,0:T(8,128)(2,1)} %spread.3), calls=%async_computation.1 | async-start | bytes 2228224 | tf_op jit(solution)/shard_map/all_to_all | solution.py:294
  44.2 21.9 %attend.2 = (bf16[128,1024]{1,0:T(8,128)(2,1)}, bf16[128,1024]{1,0:T(8,128)(2,1)}, bf16[2,128,1024]{2,1,0:T(8,128)(2,1)}, bf16[4,2,2,256,128]{4,3,2,1,0:T(8,128)...) custom-call(s32[3]{0:T(128)} %copy-done.9, bf16[128,4096]{1,0:T(8,128)(2,1)} %bitcast.34, ...), custom_call_target="tpu_custom_call" | custom-call | flops 16106127360 | bytes 4194304 | tf_op jit(solution)/shard_map/attend/pallas_call | solution.py:181
  67.1 4.2 %all-to-all-start.2 = ((bf16[4,2,2,256,128]{4,3,2,1,0:T(8,128)(2,1)}), bf16[4,2,2,256,128]{4,3,2,1,0:T(8,128)(2,1)S(1)}, u32[]{:S(2)}, u32[]{:S(2)}) async-start(bf16[4,2,2,256,128]{4,3,2,1,0:T(8,128)(2,1)} %get-tuple-element.34), calls=%async_computation.2 | async-start | bytes 2097152 | tf_op jit(solution)/shard_map/all_to_all | solution.py:294
  71.3 21.9 %attend.3 = (bf16[128,1024]{1,0:T(8,128)(2,1)}, bf16[128,1024]{1,0:T(8,128)(2,1)}, bf16[2,128,1024]{2,1,0:T(8,128)(2,1)}, bf16[4,2,2,256,128]{4,3,2,1,0:T(8,128)...) custom-call(s32[3]{0:T(128)} %copy-done.9, bf16[128,4096]{1,0:T(8,128)(2,1)} %bitcast.35, ...), custom_call_target="tpu_custom_call" | custom-call | flops 16106127360 | bytes 4194304 | tf_op jit(solution)/shard_map/attend/pallas_call | solution.py:181
  93.2 4.4 %all-to-all-start.3 = ((bf16[4,2,2,256,128]{4,3,2,1,0:T(8,128)(2,1)}), bf16[4,2,2,256,128]{4,3,2,1,0:T(8,128)(2,1)S(1)}, u32[]{:S(2)}, u32[]{:S(2)}) async-start(bf16[4,2,2,256,128]{4,3,2,1,0:T(8,128)(2,1)} %get-tuple-element.36), calls=%async_computation.3 | async-start | bytes 2097152 | tf_op jit(solution)/shard_map/all_to_all | solution.py:294
  97.6 3.4 %collective-permute-start.7 = (bf16[2,128,1024]{2,1,0:T(8,128)(2,1)}, bf16[2,128,1024]{2,1,0:T(8,128)(2,1)S(1)}, u32[]{:S(2)}, u32[]{:S(2)}) collective-permute-start(bf16[2,128,1024]{2,1,0:T(8,128)(2,1)} %get-tuple-element.29), channel_id=1, source_target_pairs={{0,1},{1,0},{2,3},{3,2},{4,5},{5,4},{6,7},{7,6},{8,9},{9,8},{10,11... | collective-permute-start | bytes 1572872 | tf_op jit(solution)/shard_map/ppermute | solution.py:289
  101.1 1.6 %collective-permute-start.9 = (f32[8,128]{1,0:T(8,128)S(1)}, f32[8,128]{1,0:T(8,128)S(1)}, u32[]{:S(2)}, u32[]{:S(2)}) collective-permute-start(f32[8,128]{1,0:T(8,128)S(1)} %copy-done.16), channel_id=1, source_target_pairs={{0,8},{1,9},{2,10},{3,11},{4,12},{5,13},{6,14},{7,15},{8,0},{9,1},... | collective-permute-start | bytes 12296 | tf_op jit(solution)/shard_map/ppermute | solution.py:289
  103.6 4.0 %collective-permute-start.10 = (f32[8,128]{1,0:T(8,128)S(1)}, f32[8,128]{1,0:T(8,128)S(1)}, u32[]{:S(2)}, u32[]{:S(2)}) collective-permute-start(f32[8,128]{1,0:T(8,128)S(1)} %add.29), channel_id=1, source_target_pairs={{0,16},{1,17},{2,18},{3,19},{4,20},{5,21},{6,22},{7,23},{8,24},{9,... | collective-permute-start | bytes 12296 | tf_op jit(solution)/shard_map/ppermute | solution.py:289
  107.6 1.4 %all-to-all-done.3.got1 = bf16[4,2,2,256,128]{4,3,2,1,0:T(8,128)(2,1)S(1)} async-done(((bf16[4,2,2,256,128]{4,3,2,1,0:T(8,128)(2,1)}), bf16[4,2,2,256,128]{4,3,2,1,0:T(8,128)(2,1)S(1)}, u32[]{:S(2)}, u32[]{:S(2)}) %all-to-all-start.3) | async-done | bytes 1048608 | tf_op jit(solution)/shard_map/all_to_all | solution.py:294
  109.0 1.1 copy-done.4
  111.2 1.3 collective-permute-start.11
  112.5 1.3 collective-permute-start.12
  113.8 4.7 %collective-permute-start.13 = (bf16[2,256,128]{2,1,0:T(8,128)(2,1)S(1)}, bf16[2,256,128]{2,1,0:T(8,128)(2,1)S(1)}, u32[]{:S(2)}, u32[]{:S(2)}) collective-permute-start(bf16[2,256,128]{2,1,0:T(8,128)(2,1)S(1)} %get-tuple-element.41), channel_id=1, source_target_pairs={{0,1},{1,0},{2,3},{3,2},{4,5},{5,4},{6,7},{7,6},{8,9},{9,8},{10,11... | collective-permute-start | bytes 393224 | tf_op jit(solution)/shard_map/ppermute | solution.py:289
  118.5 1.3 collective-permute-start.14
  119.8 1.3 collective-permute-start.15
  121.2 3.1 %rows.1 = (bf16[128,4096]{1,0:T(8,128)(2,1)}, bf16[128,4096]{1,0:T(8,128)(2,1)}) custom-call(s32[3]{0:T(128)S(1)} %copy-done.10, bf16[128,1024]{1,0:T(8,128)(2,1)S(1)} %copy-done.5, bf16[128,1024]{1,0:T(8,128)(2,1)S(1)} %copy-done.7, bf16[128,1024]{1,0:T(8,128)(2,1)S(1)} %copy-done.6, bf16[128,1024]{1,0:T(8,128)(2,1)S(1)} %copy-done.8, ...), custom_call_target="tpu_custom_call" | custom-call | tf_op jit(solution)/shard_map/rows/pallas_call | solution.py:202
  124.3 2.3 %collective-permute-done.14.refs_4_ = bf16[2,256,128]{2,1,0:T(8,128)(2,1)S(1)} collective-permute-done((bf16[2,256,128]{2,1,0:T(8,128)(2,1)S(1)}, bf16[2,256,128]{2,1,0:T(8,128)(2,1)S(1)}, u32[]{:S(2)}, u32[]{:S(2)}) %collective-permute-start.14) | collective-permute-done | bytes 131104 | tf_op jit(solution)/shard_map/ppermute | solution.py:289
  126.6 3.7 %collective-permute-done.15.refs_5_ = bf16[2,256,128]{2,1,0:T(8,128)(2,1)S(1)} collective-permute-done((bf16[2,256,128]{2,1,0:T(8,128)(2,1)S(1)}, bf16[2,256,128]{2,1,0:T(8,128)(2,1)S(1)}, u32[]{:S(2)}, u32[]{:S(2)}) %collective-permute-start.15) | collective-permute-done | bytes 131104 | tf_op jit(solution)/shard_map/ppermute | solution.py:289
  130.3 1.3 %final.1 = (bf16[128,512]{1,0:T(8,128)(2,1)}, bf16[128,512]{1,0:T(8,128)(2,1)}) custom-call(s32[3]{0:T(128)S(1)} %copy-done.10, f32[8,128]{1,0:T(8,128)S(1)} %add.30.tally_ref, f32[2,256,128]{2,1,0:T(8,128)S(1)} %get-tuple-element.38.refs_0_, bf16[2,256,128]{2,1,0:T(8,128)(2,1)S(1)} %collective-permute-done.11.refs_1_, ...), custom_call_target="tpu_custom_call" | custom-call | tf_op jit(solution)/shard_map/final/pallas_call | solution.py:202
  (77 shorter events, 13.8 us)
Async XLA Ops:
  2.9 10.8 %copy-start.14 = (bf16[1,128,4096]{2,1,0:T(8,128)(2,1)S(1)}, bf16[1,128,4096]{2,1,0:T(8,128)(2,1)}, u32[]{:S(2)}) copy-start(bf16[1,128,4096]{2,1,0:T(8,128)(2,1)} %param.6) | copy-start | bytes 3145732
  4.1 2.5 %collective-permute-start.2 = (bf16[2,272,128]{2,1,0:T(8,128)(2,1)S(1)}, bf16[2,272,128]{2,1,0:T(8,128)(2,1)S(1)}, u32[]{:S(2)}, u32[]{:S(2)}) collective-permute-start(bf16[2,272,128]{2,1,0:T(8,128)(2,1)S(1)} %get-tuple-element.51), channel_id=1, source_target_pairs={{0,1},{1,0},{2,3},{3,2},{4,5},{5,4},{6,7},{7,6},{8,9},{9,8},{10,11... | collective-permute-start | bytes 417800 | tf_op jit(solution)/shard_map/ppermute | solution.py:289
  6.7 31.2 %copy-start = (bf16[2,2,272,128]{3,2,1,0:T(8,128)(2,1)}, bf16[2,2,272,128]{3,2,1,0:T(8,128)(2,1)S(1)}, u32[]{:S(2)}) copy-start(bf16[2,2,272,128]{3,2,1,0:T(8,128)(2,1)S(1)} %pad_maximum_fusion.own_ref) | copy-start | bytes 835588
  6.7 10.6 %collective-permute-start.3 = (bf16[2,2,272,128]{3,2,1,0:T(8,128)(2,1)S(1)}, bf16[2,2,272,128]{3,2,1,0:T(8,128)(2,1)S(1)}, u32[]{:S(2)}, u32[]{:S(2)}) collective-permute-start(bf16[2,2,272,128]{3,2,1,0:T(8,128)(2,1)S(1)} %pad_maximum_fusion.own_ref), channel_id=1, source_target_pairs={{0,8},{1,9},{2,10},{3,11},{4,12},{5,13},{6,14},{7,15},{8,16},{9,17... | collective-permute-start | bytes 835592 | tf_op jit(solution)/shard_map/ppermute | solution.py:289
  8.5 11.8 %collective-permute-start.4 = (bf16[2,2,272,128]{3,2,1,0:T(8,128)(2,1)S(1)}, bf16[2,2,272,128]{3,2,1,0:T(8,128)(2,1)S(1)}, u32[]{:S(2)}, u32[]{:S(2)}) collective-permute-start(bf16[2,2,272,128]{3,2,1,0:T(8,128)(2,1)S(1)} %pad_maximum_fusion.own_ref), channel_id=1, source_target_pairs={{0,16},{1,17},{2,18},{3,19},{4,20},{5,21},{6,22},{7,23},{8,24},{9,... | collective-permute-start | bytes 835592 | tf_op jit(solution)/shard_map/ppermute | solution.py:289
  14.5 29.6 %collective-permute-start = (bf16[128,2048]{1,0:T(8,128)(2,1)}, bf16[128,2048]{1,0:T(8,128)(2,1)}, u32[]{:S(2)}, u32[]{:S(2)}) collective-permute-start(bf16[128,2048]{1,0:T(8,128)(2,1)} %dynamic-slice_bitcast_fusion.1), channel_id=1, source_target_pairs={{0,1},{1,0},{2,3},{3,2},{4,5},{5,4},{6,7},{7,6},{8,9},{9,8},{10,11... | collective-permute-start | bytes 1572872 | tf_op jit(solution)/shard_map/ppermute | solution.py:289
  15.5 22.4 %copy-start.9 = (s32[3]{0:T(128)}, s32[3]{0:T(128)S(1)}, u32[]{:S(2)}) copy-start(s32[3]{0:T(128)S(1)} %pad_add_fusion.s_ref) | copy-start | bytes 40
  17.3 20.6 %copy-start.1 = (bf16[2,2,272,128]{3,2,1,0:T(8,128)(2,1)}, bf16[2,2,272,128]{3,2,1,0:T(8,128)(2,1)S(1)}, u32[]{:S(2)}) copy-start(bf16[2,2,272,128]{3,2,1,0:T(8,128)(2,1)S(1)} %collective-permute-done.3.za_ref) | copy-start | bytes 835588
  20.2 17.7 %copy-start.2 = (bf16[2,2,272,128]{3,2,1,0:T(8,128)(2,1)}, bf16[2,2,272,128]{3,2,1,0:T(8,128)(2,1)S(1)}, u32[]{:S(2)}) copy-start(bf16[2,2,272,128]{3,2,1,0:T(8,128)(2,1)S(1)} %collective-permute-done.4.zc_ref) | copy-start | bytes 835588
  21.9 18.7 %all-to-all-start = ((bf16[4,2,2,272,128]{4,3,2,1,0:T(8,128)(2,1)}), bf16[4,2,2,272,128]{4,3,2,1,0:T(8,128)(2,1)S(1)}, u32[]{:S(2)}, u32[]{:S(2)}) async-start(bf16[4,2,2,272,128]{4,3,2,1,0:T(8,128)(2,1)} %spread.2), calls=%async_computation | async-start | bytes 2228224 | tf_op jit(solution)/shard_map/all_to_all | solution.py:294
  27.0 17.1 %collective-permute-start.1 = (bf16[128,2048]{1,0:T(8,128)(2,1)}, bf16[128,2048]{1,0:T(8,128)(2,1)}, u32[]{:S(2)}, u32[]{:S(2)}) collective-permute-start(bf16[128,2048]{1,0:T(8,128)(2,1)} %dynamic-slice_bitcast_fusion), channel_id=1, source_target_pairs={{0,1},{1,0},{2,3},{3,2},{4,5},{5,4},{6,7},{7,6},{8,9},{9,8},{10,11... | collective-permute-start | bytes 1572872 | tf_op jit(solution)/shard_map/ppermute | solution.py:289
  29.7 2.8 %collective-permute-start.5 = (f32[8,128]{1,0:T(8,128)S(1)}, f32[8,128]{1,0:T(8,128)S(1)}, u32[]{:S(2)}, u32[]{:S(2)}) collective-permute-start(f32[8,128]{1,0:T(8,128)S(1)} %broadcast_in_dim.28), channel_id=1, source_target_pairs={{0,32},{32,0},{64,96},{96,64},{1,33},{33,1},{65,97},{97,65},{2,34}... | collective-permute-start | bytes 12296 | tf_op jit(solution)/shard_map/ppermute | solution.py:310
  33.2 4.0 %collective-permute-start.6 = (f32[8,128]{1,0:T(8,128)S(1)}, f32[8,128]{1,0:T(8,128)S(1)}, u32[]{:S(2)}, u32[]{:S(2)}) collective-permute-start(f32[8,128]{1,0:T(8,128)S(1)} %broadcast_add_fusion), channel_id=1, source_target_pairs={{0,64},{32,96},{64,0},{96,32},{1,65},{33,97},{65,1},{97,33},{2,66}... | collective-permute-start | bytes 12296 | tf_op jit(solution)/shard_map/ppermute | solution.py:310
  40.6 25.4 %all-to-all-start.1 = ((bf16[4,2,2,272,128]{4,3,2,1,0:T(8,128)(2,1)}), bf16[4,2,2,272,128]{4,3,2,1,0:T(8,128)(2,1)S(1)}, u32[]{:S(2)}, u32[]{:S(2)}) async-start(bf16[4,2,2,272,128]{4,3,2,1,0:T(8,128)(2,1)} %spread.3), calls=%async_computation.1 | async-start | bytes 2228224 | tf_op jit(solution)/shard_map/all_to_all | solution.py:294
  67.1 26.1 %all-to-all-start.2 = ((bf16[4,2,2,256,128]{4,3,2,1,0:T(8,128)(2,1)}), bf16[4,2,2,256,128]{4,3,2,1,0:T(8,128)(2,1)S(1)}, u32[]{:S(2)}, u32[]{:S(2)}) async-start(bf16[4,2,2,256,128]{4,3,2,1,0:T(8,128)(2,1)} %get-tuple-element.34), calls=%async_computation.2 | async-start | bytes 2097152 | tf_op jit(solution)/shard_map/all_to_all | solution.py:294
  93.2 7.9 %copy-start.16 = (f32[8,128]{1,0:T(8,128)S(1)}, f32[8,128]{1,0:T(8,128)}, u32[]{:S(2)}) copy-start(f32[8,128]{1,0:T(8,128)} %get-tuple-element.31) | copy-start | bytes 12292
  93.2 15.8 %copy-start.3 = (f32[3,2,256,128]{3,2,1,0:T(8,128)S(1)}, f32[3,2,256,128]{3,2,1,0:T(8,128)}, u32[]{:S(2)}) copy-start(f32[3,2,256,128]{3,2,1,0:T(8,128)} %get-tuple-element.35.loc0) | copy-start | bytes 2359300
  93.2 15.8 %copy-start.10 = (s32[3]{0:T(128)S(1)}, s32[3]{0:T(128)}, u32[]{:S(2)}) copy-start(s32[3]{0:T(128)} %copy-done.9) | copy-start | bytes 40
  93.2 15.8 %all-to-all-start.3 = ((bf16[4,2,2,256,128]{4,3,2,1,0:T(8,128)(2,1)}), bf16[4,2,2,256,128]{4,3,2,1,0:T(8,128)(2,1)S(1)}, u32[]{:S(2)}, u32[]{:S(2)}) async-start(bf16[4,2,2,256,128]{4,3,2,1,0:T(8,128)(2,1)} %get-tuple-element.36), calls=%async_computation.3 | async-start | bytes 2097152 | tf_op jit(solution)/shard_map/all_to_all | solution.py:294
  97.6 20.9 %collective-permute-start.7 = (bf16[2,128,1024]{2,1,0:T(8,128)(2,1)}, bf16[2,128,1024]{2,1,0:T(8,128)(2,1)S(1)}, u32[]{:S(2)}, u32[]{:S(2)}) collective-permute-start(bf16[2,128,1024]{2,1,0:T(8,128)(2,1)} %get-tuple-element.29), channel_id=1, source_target_pairs={{0,1},{1,0},{2,3},{3,2},{4,5},{5,4},{6,7},{7,6},{8,9},{9,8},{10,11... | collective-permute-start | bytes 1572872 | tf_op jit(solution)/shard_map/ppermute | solution.py:289
  101.1 18.7 %collective-permute-start.8 = (bf16[2,128,1024]{2,1,0:T(8,128)(2,1)}, bf16[2,128,1024]{2,1,0:T(8,128)(2,1)}, u32[]{:S(2)}, u32[]{:S(2)}) collective-permute-start(bf16[2,128,1024]{2,1,0:T(8,128)(2,1)} %get-tuple-element.30), channel_id=1, source_target_pairs={{0,1},{1,0},{2,3},{3,2},{4,5},{5,4},{6,7},{7,6},{8,9},{9,8},{10,11... | collective-permute-start | bytes 1572872 | tf_op jit(solution)/shard_map/ppermute | solution.py:289
  101.1 2.6 %collective-permute-start.9 = (f32[8,128]{1,0:T(8,128)S(1)}, f32[8,128]{1,0:T(8,128)S(1)}, u32[]{:S(2)}, u32[]{:S(2)}) collective-permute-start(f32[8,128]{1,0:T(8,128)S(1)} %copy-done.16), channel_id=1, source_target_pairs={{0,8},{1,9},{2,10},{3,11},{4,12},{5,13},{6,14},{7,15},{8,0},{9,1},... | collective-permute-start | bytes 12296 | tf_op jit(solution)/shard_map/ppermute | solution.py:289
  103.6 10.1 %collective-permute-start.10 = (f32[8,128]{1,0:T(8,128)S(1)}, f32[8,128]{1,0:T(8,128)S(1)}, u32[]{:S(2)}, u32[]{:S(2)}) collective-permute-start(f32[8,128]{1,0:T(8,128)S(1)} %add.29), channel_id=1, source_target_pairs={{0,16},{1,17},{2,18},{3,19},{4,20},{5,21},{6,22},{7,23},{8,24},{9,... | collective-permute-start | bytes 12296 | tf_op jit(solution)/shard_map/ppermute | solution.py:289
  110.2 11.0 %copy-start.5 = (bf16[128,1024]{1,0:T(8,128)(2,1)S(1)}, bf16[128,1024]{1,0:T(8,128)(2,1)}, u32[]{:S(2)}) copy-start(bf16[128,1024]{1,0:T(8,128)(2,1)} %get-tuple-element.25.oo0) | copy-start | bytes 786436
  110.2 11.0 %copy-start.6 = (bf16[128,1024]{1,0:T(8,128)(2,1)S(1)}, bf16[128,1024]{1,0:T(8,128)(2,1)}, u32[]{:S(2)}) copy-start(bf16[128,1024]{1,0:T(8,128)(2,1)} %get-tuple-element.27.dq0) | copy-start | bytes 786436
  110.2 11.0 %copy-start.7 = (bf16[128,1024]{1,0:T(8,128)(2,1)S(1)}, bf16[128,1024]{1,0:T(8,128)(2,1)}, u32[]{:S(2)}) copy-start(bf16[128,1024]{1,0:T(8,128)(2,1)} %get-tuple-element.26.oo1) | copy-start | bytes 786436
  110.2 11.0 %copy-start.8 = (bf16[128,1024]{1,0:T(8,128)(2,1)S(1)}, bf16[128,1024]{1,0:T(8,128)(2,1)}, u32[]{:S(2)}) copy-start(bf16[128,1024]{1,0:T(8,128)(2,1)} %get-tuple-element.28.dq1) | copy-start | bytes 786436
  111.2 13.1 %collective-permute-start.11 = (bf16[2,256,128]{2,1,0:T(8,128)(2,1)S(1)}, bf16[2,256,128]{2,1,0:T(8,128)(2,1)S(1)}, u32[]{:S(2)}, u32[]{:S(2)}) collective-permute-start(bf16[2,256,128]{2,1,0:T(8,128)(2,1)S(1)} %get-tuple-element.39), channel_id=1, source_target_pairs={{8,0},{9,1},{10,2},{11,3},{12,4},{13,5},{14,6},{15,7},{16,8},{17,9... | collective-permute-start | bytes 393224 | tf_op jit(solution)/shard_map/ppermute | solution.py:289
  112.5 11.8 %collective-permute-start.12 = (bf16[2,256,128]{2,1,0:T(8,128)(2,1)S(1)}, bf16[2,256,128]{2,1,0:T(8,128)(2,1)S(1)}, u32[]{:S(2)}, u32[]{:S(2)}) collective-permute-start(bf16[2,256,128]{2,1,0:T(8,128)(2,1)S(1)} %get-tuple-element.40), channel_id=1, source_target_pairs={{16,0},{17,1},{18,2},{19,3},{20,4},{21,5},{22,6},{23,7},{24,8},{25... | collective-permute-start | bytes 393224 | tf_op jit(solution)/shard_map/ppermute | solution.py:289
  113.8 10.5 %collective-permute-start.13 = (bf16[2,256,128]{2,1,0:T(8,128)(2,1)S(1)}, bf16[2,256,128]{2,1,0:T(8,128)(2,1)S(1)}, u32[]{:S(2)}, u32[]{:S(2)}) collective-permute-start(bf16[2,256,128]{2,1,0:T(8,128)(2,1)S(1)} %get-tuple-element.41), channel_id=1, source_target_pairs={{0,1},{1,0},{2,3},{3,2},{4,5},{5,4},{6,7},{7,6},{8,9},{9,8},{10,11... | collective-permute-start | bytes 393224 | tf_op jit(solution)/shard_map/ppermute | solution.py:289
  118.5 8.1 %collective-permute-start.14 = (bf16[2,256,128]{2,1,0:T(8,128)(2,1)S(1)}, bf16[2,256,128]{2,1,0:T(8,128)(2,1)S(1)}, u32[]{:S(2)}, u32[]{:S(2)}) collective-permute-start(bf16[2,256,128]{2,1,0:T(8,128)(2,1)S(1)} %get-tuple-element.42), channel_id=1, source_target_pairs={{8,1},{9,0},{10,3},{11,2},{12,5},{13,4},{14,7},{15,6},{16,9},{17,8... | collective-permute-start | bytes 393224 | tf_op jit(solution)/shard_map/ppermute | solution.py:289
  119.8 10.5 %collective-permute-start.15 = (bf16[2,256,128]{2,1,0:T(8,128)(2,1)S(1)}, bf16[2,256,128]{2,1,0:T(8,128)(2,1)S(1)}, u32[]{:S(2)}, u32[]{:S(2)}) collective-permute-start(bf16[2,256,128]{2,1,0:T(8,128)(2,1)S(1)} %get-tuple-element.43), channel_id=1, source_target_pairs={{16,1},{17,0},{18,3},{19,2},{20,5},{21,4},{22,7},{23,6},{24,9},{25... | collective-permute-start | bytes 393224 | tf_op jit(solution)/shard_map/ppermute | solution.py:289
  (5 other events, 12.7 us)

commit v2 on v1

--- a/solution.py
+++ b/solution.py
@@ -49,8 +49,35 @@
     lax.fori_loop(0, 4, pair, 0)
 
 
-def attend_kernel(s_ref, qo_ref, qs_ref, go_ref, gs_ref, own_ref, za_ref, zc_ref, y_ref, tally_ref,
-                  oo_ref, dqo_ref, swap_ref, p_ref, loc_ref, cnt_ref, kk, vv, kt, vt, bias, sc, pp, ds, dka, dva):
+def run_ahead(score, weigh, output, dscore, dvalue, dkey, dquery, start):
+    R = range(NB)
+    S = [start(h) for h in range(8)]
+    for b in R:
+        score(0, S[0], b)
+    for b in R:
+        weigh(0, S[0], b)
+    for b in R:
+        score(1, S[1], b)
+    for h in range(8):
+        t, u = h % 2, (h + 1) % 2
+        output(t, S[h])
+        for b in R:
+            dscore(t, S[h], b)
+            if h < 7:
+                weigh(u, S[h + 1], b)
+        for b in R:
+            dvalue(t, S[h], b)
+            dkey(t, S[h], b)
+            if h < 6:
+                score(t, S[h + 2], b)
+        dquery(t, S[h])
+
+
+def attend_kernel(ahead, s_ref, qo_ref, qs_ref, go_ref, gs_ref, own_ref, za_ref, zc_ref, y_ref, tally_ref,
+                  oo_ref, dqo_ref, swap_ref, *refs):
+    n_parts = 1 if ahead else 3
+    p_refs = refs[:n_parts]
+    loc_ref, cnt_ref, kk, vv, kt, vt, bias, sc, pp, ds, dka, dva = refs[n_parts:]
     core, z, y = s_ref[0], s_ref[1], s_ref[2]
     chip = 4 * z + y
     blocks = [(own_ref, (), None), (za_ref, (), chip - 4), (zc_ref, (), chip - 8)]
@@ -142,7 +169,7 @@
         st["cols"], st["q"], st["g"] = load(h)
         return st
 
-    run_heads(score, weigh, output, dscore, dvalue, dkey, dquery, start)
+    (run_ahead if ahead else run_heads)(score, weigh, output, dscore, dvalue, dkey, dquery, start)
     tally = tally_ref[...]
     for s in (1, 2, 3):
         digits = y_ref[(y - s) & 3, 0, 0, 256:272].astype(F32)
@@ -155,9 +182,10 @@
                 loc_ref[b, o, 0:128] = dka[rows]
                 loc_ref[b, o, 128:256] = dva[rows]
             else:
-                turned = (y - (b - 1) // 2) & 3
-                p_ref[turned, (b - 3) % 2, o, 0:128] = dka[rows].astype(BF)
-                p_ref[turned, (b - 3) % 2, o, 128:256] = dva[rows].astype(BF)
+                s = (b - 1) // 2
+                ref, at = (p_refs[0], ((y - s) & 3,)) if ahead else (p_refs[s - 1], ())
+                ref[at + ((b - 3) % 2, o, slice(0, 128))] = dka[rows].astype(BF)
+                ref[at + ((b - 3) % 2, o, slice(128, 256))] = dva[rows].astype(BF)
 
 
 def whole(a):
@@ -175,11 +203,13 @@
     rows = jax.ShapeDtypeStruct((128, 1024), BF)
     pair = jax.ShapeDtypeStruct((2, 128, 1024), BF)
     loc = jax.ShapeDtypeStruct((3, 2, 256, 128), F32)
-    outs = [rows, rows, pair, jax.ShapeDtypeStruct((4, 2, 2, 256, 128), BF), loc, jax.ShapeDtypeStruct((8, 128), F32)]
+    part = jax.ShapeDtypeStruct((2, 2, 256, 128), BF)
+    parts = [jax.ShapeDtypeStruct((4, 2, 2, 256, 128), BF)] if j else [part] * 3
+    outs = [rows, rows, pair, *parts, loc, jax.ShapeDtypeStruct((8, 128), F32)]
     n = NB * 256
     ins = (own, za, zc, ys, tally)
     return pl.pallas_call(
-        attend_kernel,
+        functools.partial(attend_kernel, j == 1),
         out_shape=outs,
         grid_spec=pltpu.PrefetchScalarGridSpec(
             num_scalar_prefetch=1,
@@ -233,14 +263,15 @@
             out_ref[t, 1] = zc_ref[...]
 
 
-def sum_kernel(s_ref, got0, loc0, got1, loc1, a_mine, a_theirs, c_mine, c_theirs, here, here_theirs):
+def sum_kernel(s_ref, got01, got02, got03, loc0, got1, loc1, a_mine, a_theirs, c_mine, c_theirs, here, here_theirs):
     y = s_ref[2]
-    for j, (got, loc_ref) in enumerate(((got0, loc0), (got1, loc1))):
+    for j, (got, loc_ref) in enumerate((((got01, got02, got03), loc0), (got1, loc1))):
         a, c, h = loc_ref[1], loc_ref[2], loc_ref[0]
         for s in (1, 2, 3):
-            t = (y + s) & 3
-            a = a + got[t, 0].astype(F32)
-            b = got[t, 1].astype(F32)
+            at = ((y + s) & 3,) if j else ()
+            r = got if j else got[s - 1]
+            a = a + r[at + (0,)].astype(F32)
+            b = r[at + (1,)].astype(F32)
             h = h + jnp.where(y + s < 4, b, 0.0)
             c = c + jnp.where(y + s < 4, 0.0, b)
         a_mine[j] = a[0].astype(BF)
@@ -317,12 +348,12 @@
     ]
 
     to = lambda x, a, c: send(x, lambda z, yy, cc: (z + a, yy, cc + c))
-    oo0, dq0, pair0, part0, loc0, _ = attend(scal, 0, q, qs, g, gs, own, za, zc, ys[0], counted)
-    got0 = trade_y(part0)
+    oo0, dq0, pair0, *parts, loc0, _ = attend(scal, 0, q, qs, g, gs, own, za, zc, ys[0], counted)
+    got0 = [send(p, lambda z, y, c: (z, y - s, c)) for s, p in zip((1, 2, 3), parts)]
     oo1, dq1, pair1, part1, loc1, tally = attend(scal, 1, q, qs, g, gs, own, za, zc, ys[1], counted)
     sides, sides32 = kind((2, 256, 128), BF), kind((2, 256, 128), F32)
     a_mine, a_theirs, c_mine, c_theirs, here, here_theirs = small(
-        sum_kernel, scal, (got0, loc0, trade_y(part1), loc1), [sides] * 4 + [sides32, sides], "sum"
+        sum_kernel, scal, (*got0, loc0, trade_y(part1), loc1), [sides] * 4 + [sides32, sides], "sum"
     )
     kv = (here, to(a_mine, -1, 0), to(c_mine, -2, 0), swap(here_theirs), to(a_theirs, -1, 1), to(c_theirs, -2, 1))
     for step in (1, 2):

time: 133 us -> 143 us (1.075)
  waiting for transfers between devices: 17.9 us -> 34.6 us
  starting transfers between devices: 50.2 us -> 44.4 us
  Pallas kernels: 52.5 us -> 49.8 us
    ppermute x14 -> x17, waiting for transfers between devices: 12.7 us -> 27.2 us  [send(): return lax.ppermute(x, 'ctx', pairs)]
    all_to_all x4 -> x3, starting transfers between devices: 16.4 us -> 11.9 us  [shard(): lax.all_to_all(x, 'ctx', 0, 0, axis_index_groups=rows_of_y)]
    all_to_all x4 -> x3, waiting for transfers between devices: 2.49 us -> 5.98 us  [shard(): lax.all_to_all(x, 'ctx', 0, 0, axis_index_groups=rows_of_y)]
    pallas_call x2, Pallas kernels: 43.8 us -> 42.1 us  [attend(): pl.pallas_call(functools.partial(attend_kernel, j == 1), out_shape=outs,...]
    unnamed x38 -> x40, local copies, waits for them, and re-layouts: 2.66 us -> 4.34 us
    ppermute x14 -> x17, starting transfers between devices: 29.7 us -> 28.7 us  [send(): return lax.ppermute(x, 'ctx', pairs)]
  transfers between devices with their start and end apart: 20 -> 22, of which waited for: 10 -> 9; matrix products, arithmetic and copies ran while one was open for 3% -> 2% of each run, Pallas kernels for 39% -> 33%
where the time goes in v2:
time: 143 us; the launch traced here: 141 us
  Pallas kernels  49.8 us (35%)
  starting transfers between devices  44.4 us (31%)
  waiting for transfers between devices  34.6 us (24%)
  local copies, waits for them, and re-layouts  7.73 us (5%)
  other arithmetic  3.43 us (2%)
    pallas_call x2, Pallas kernels, attend(): pl.pallas_call(functools.partial(attend_kernel, j == 1), out_shape=outs,...  42.1 us
    ppermute x17, starting transfers between devices, send(): return lax.ppermute(x, 'ctx', pairs)  28.7 us
    ppermute x17, waiting for transfers between devices, send(): return lax.ppermute(x, 'ctx', pairs)  27.2 us
    all_to_all x3, starting transfers between devices, shard(): lax.all_to_all(x, 'ctx', 0, 0, axis_index_groups=rows_of_y)  11.9 us
    pallas_call x5, Pallas kernels, small(): pl.pallas_call(kernel, out_shape=outs, grid_spec=pltpu.PrefetchScalarGrid...  7.73 us
    all_to_all x3, waiting for transfers between devices, shard(): lax.all_to_all(x, 'ctx', 0, 0, axis_index_groups=rows_of_y)  5.98 us
    unnamed x40, local copies, waits for them, and re-layouts  4.34 us
    ppermute x2, starting transfers between devices, shard(): lax.ppermute(counted, 'dp', [(i, i ^ step) for i in range(4)])  3.82 us
  transfers between devices with their start and end apart: 22, of which 9 were waited for; matrix products, arithmetic and copies ran while one was open for 2% of the time, Pallas kernels for 33%

profile of v2, /device:TPU:1, one launch (start us, length us, event | category | flops | bytes accessed | tf_op | source)
XLA Modules:
  0.0 141.0 jit_solution(1697871433531732886)
XLA Ops:
  4.1 1.5 %collective-permute-start.2 = (bf16[2,272,128]{2,1,0:T(8,128)(2,1)S(1)}, bf16[2,272,128]{2,1,0:T(8,128)(2,1)S(1)}, u32[]{:S(2)}, u32[]{:S(2)}) collective-permute-start(bf16[2,272,128]{2,1,0:T(8,128)(2,1)S(1)} %get-tuple-element.55), channel_id=1, source_target_pairs={{0,1},{1,0},{2,3},{3,2},{4,5},{5,4},{6,7},{7,6},{8,9},{9,8},{10,11... | collective-permute-start | bytes 417800 | tf_op jit(solution)/shard_map/ppermute | solution.py:320
  6.7 1.8 %collective-permute-start.3 = (bf16[2,2,272,128]{3,2,1,0:T(8,128)(2,1)S(1)}, bf16[2,2,272,128]{3,2,1,0:T(8,128)(2,1)S(1)}, u32[]{:S(2)}, u32[]{:S(2)}) collective-permute-start(bf16[2,2,272,128]{3,2,1,0:T(8,128)(2,1)S(1)} %pad_maximum_fusion.own_ref), channel_id=1, source_target_pairs={{0,8},{1,9},{2,10},{3,11},{4,12},{5,13},{6,14},{7,15},{8,16},{9,17... | collective-permute-start | bytes 835592 | tf_op jit(solution)/shard_map/ppermute | solution.py:320
  8.4 8.9 %collective-permute-done.3.za_ref = bf16[2,2,272,128]{3,2,1,0:T(8,128)(2,1)S(1)} collective-permute-done((bf16[2,2,272,128]{3,2,1,0:T(8,128)(2,1)S(1)}, bf16[2,2,272,128]{3,2,1,0:T(8,128)(2,1)S(1)}, u32[]{:S(2)}, u32[]{:S(2)}) %collective-permute-start.3) | collective-permute-done | bytes 278560 | tf_op jit(solution)/shard_map/ppermute | solution.py:320
  18.6 1.3 collective-permute-start.5
  19.9 2.9 %collective-permute-start.4 = (bf16[2,2,272,128]{3,2,1,0:T(8,128)(2,1)S(1)}, bf16[2,2,272,128]{3,2,1,0:T(8,128)(2,1)S(1)}, u32[]{:S(2)}, u32[]{:S(2)}) collective-permute-start(bf16[2,2,272,128]{3,2,1,0:T(8,128)(2,1)S(1)} %pad_maximum_fusion.own_ref), channel_id=1, source_target_pairs={{0,16},{1,17},{2,18},{3,19},{4,20},{5,21},{6,22},{7,23},{8,24},{9,... | collective-permute-start | bytes 835592 | tf_op jit(solution)/shard_map/ppermute | solution.py:320
  23.4 2.5 %collective-permute-start.6 = (f32[8,128]{1,0:T(8,128)S(1)}, f32[8,128]{1,0:T(8,128)S(1)}, u32[]{:S(2)}, u32[]{:S(2)}) collective-permute-start(f32[8,128]{1,0:T(8,128)S(1)} %broadcast_add_fusion), channel_id=1, source_target_pairs={{0,64},{32,96},{64,0},{96,32},{1,65},{33,97},{65,1},{97,33},{2,66}... | collective-permute-start | bytes 12296 | tf_op jit(solution)/shard_map/ppermute | solution.py:341
  26.0 1.4 %collective-permute-done.6 = f32[8,128]{1,0:T(8,128)S(1)} collective-permute-done((f32[8,128]{1,0:T(8,128)S(1)}, f32[8,128]{1,0:T(8,128)S(1)}, u32[]{:S(2)}, u32[]{:S(2)}) %collective-permute-start.6) | collective-permute-done | bytes 4128 | tf_op jit(solution)/shard_map/ppermute | solution.py:341
  28.2 1.7 %spread.3 = bf16[4,2,2,272,128]{4,3,2,1,0:T(8,128)(2,1)} custom-call(s32[3]{0:T(128)S(1)} %pad_add_fusion.s_ref, bf16[2,2,272,128]{3,2,1,0:T(8,128)(2,1)S(1)} %pad_maximum_fusion.own_ref, bf16[2,2,272,128]{3,2,1,0:T(8,128)(2,1)S(1)} %collective-permute-done.3.za_ref, bf16[2,2,272,128]{3,2,1,0:T(8,128)(2,1)S(1)} %collective-permute-done.4.zc_ref, ...), custom_call_target="tpu_custom_call" | custom-call | tf_op jit(solution)/shard_map/spread/pallas_call | solution.py:232
  29.8 4.2 %all-to-all-start.1 = ((bf16[4,2,2,272,128]{4,3,2,1,0:T(8,128)(2,1)}), bf16[4,2,2,272,128]{4,3,2,1,0:T(8,128)(2,1)S(1)}, u32[]{:S(2)}, u32[]{:S(2)}) async-start(bf16[4,2,2,272,128]{4,3,2,1,0:T(8,128)(2,1)} %spread.3), calls=%async_computation.1 | async-start | bytes 2228224 | tf_op jit(solution)/shard_map/all_to_all | solution.py:325
  34.0 1.2 dynamic-slice_bitcast_fusion
  35.2 3.3 %collective-permute-start.1 = (bf16[128,2048]{1,0:T(8,128)(2,1)S(1)}, bf16[128,2048]{1,0:T(8,128)(2,1)}, u32[]{:S(2)}, u32[]{:S(2)}) collective-permute-start(bf16[128,2048]{1,0:T(8,128)(2,1)S(1)} %dynamic-slice_bitcast_fusion), channel_id=1, source_target_pairs={{0,1},{1,0},{2,3},{3,2},{4,5},{5,4},{6,7},{7,6},{8,9},{9,8},{10,11... | collective-permute-start | bytes 1572872 | tf_op jit(solution)/shard_map/ppermute | solution.py:320
  38.7 1.7 %spread.2 = bf16[4,2,2,272,128]{4,3,2,1,0:T(8,128)(2,1)} custom-call(s32[3]{0:T(128)S(1)} %pad_add_fusion.s_ref, bf16[2,2,272,128]{3,2,1,0:T(8,128)(2,1)S(1)} %pad_maximum_fusion.own_ref, bf16[2,2,272,128]{3,2,1,0:T(8,128)(2,1)S(1)} %collective-permute-done.3.za_ref, bf16[2,2,272,128]{3,2,1,0:T(8,128)(2,1)S(1)} %collective-permute-done.4.zc_ref, ...), custom_call_target="tpu_custom_call" | custom-call | tf_op jit(solution)/shard_map/spread/pallas_call | solution.py:232
  40.4 6.0 %all-to-all-done.1.y_ref = bf16[4,2,2,272,128]{4,3,2,1,0:T(8,128)(2,1)S(1)} async-done(((bf16[4,2,2,272,128]{4,3,2,1,0:T(8,128)(2,1)}), bf16[4,2,2,272,128]{4,3,2,1,0:T(8,128)(2,1)S(1)}, u32[]{:S(2)}, u32[]{:S(2)}) %all-to-all-start.1) | async-done | bytes 1114144 | tf_op jit(solution)/shard_map/all_to_all | solution.py:325
  47.4 3.7 %all-to-all-start = ((bf16[4,2,2,272,128]{4,3,2,1,0:T(8,128)(2,1)}), bf16[4,2,2,272,128]{4,3,2,1,0:T(8,128)(2,1)S(1)}, u32[]{:S(2)}, u32[]{:S(2)}) async-start(bf16[4,2,2,272,128]{4,3,2,1,0:T(8,128)(2,1)} %spread.2), calls=%async_computation | async-start | bytes 2228224 | tf_op jit(solution)/shard_map/all_to_all | solution.py:325
  51.1 20.1 %attend.3 = (bf16[128,1024]{1,0:T(8,128)(2,1)}, bf16[128,1024]{1,0:T(8,128)(2,1)}, bf16[2,128,1024]{2,1,0:T(8,128)(2,1)}, bf16[4,2,2,256,128]{4,3,2,1,0:T(8,128)...) custom-call(s32[3]{0:T(128)} %copy-done.11, bf16[128,4096]{1,0:T(8,128)(2,1)} %bitcast.34, ...), custom_call_target="tpu_custom_call" | custom-call | flops 16106127360 | bytes 4194304 | tf_op jit(solution)/shard_map/attend/pallas_call | solution.py:211
  71.3 4.0 %all-to-all-start.2 = ((bf16[4,2,2,256,128]{4,3,2,1,0:T(8,128)(2,1)}), bf16[4,2,2,256,128]{4,3,2,1,0:T(8,128)(2,1)S(1)}, u32[]{:S(2)}, u32[]{:S(2)}) async-start(bf16[4,2,2,256,128]{4,3,2,1,0:T(8,128)(2,1)} %get-tuple-element.40), calls=%async_computation.2 | async-start | bytes 2097152 | tf_op jit(solution)/shard_map/all_to_all | solution.py:325
  75.3 22.0 %attend.2 = (bf16[128,1024]{1,0:T(8,128)(2,1)}, bf16[128,1024]{1,0:T(8,128)(2,1)}, bf16[2,128,1024]{2,1,0:T(8,128)(2,1)}, bf16[2,2,256,128]{3,2,1,0:T(8,128)(2,1...) custom-call(s32[3]{0:T(128)} %copy-done.11, ...), custom_call_target="tpu_custom_call" | custom-call | flops 16106127360 | bytes 4194304 | tf_op jit(solution)/shard_map/attend/pallas_call | solution.py:211
  97.3 5.0 %collective-permute-start.7 = (bf16[2,128,1024]{2,1,0:T(8,128)(2,1)}, bf16[2,128,1024]{2,1,0:T(8,128)(2,1)S(1)}, u32[]{:S(2)}, u32[]{:S(2)}) collective-permute-start(bf16[2,128,1024]{2,1,0:T(8,128)(2,1)} %get-tuple-element.31), channel_id=1, source_target_pairs={{0,1},{1,0},{2,3},{3,2},{4,5},{5,4},{6,7},{7,6},{8,9},{9,8},{10,11... | collective-permute-start | bytes 1572872 | tf_op jit(solution)/shard_map/ppermute | solution.py:320
  103.1 2.9 %collective-permute-start.11 = (bf16[2,2,256,128]{3,2,1,0:T(8,128)(2,1)}, bf16[2,2,256,128]{3,2,1,0:T(8,128)(2,1)S(1)}, u32[]{:S(2)}, u32[]{:S(2)}) collective-permute-start(bf16[2,2,256,128]{3,2,1,0:T(8,128)(2,1)} %get-tuple-element.36), channel_id=1, source_target_pairs={{0,6},{1,7},{2,0},{3,1},{4,2},{5,3},{6,4},{7,5},{8,14},{9,15},{10,... | collective-permute-start | bytes 786440 | tf_op jit(solution)/shard_map/ppermute | solution.py:320
  107.2 4.8 %collective-permute-done.11.got01 = bf16[2,2,256,128]{3,2,1,0:T(8,128)(2,1)S(1)} collective-permute-done((bf16[2,2,256,128]{3,2,1,0:T(8,128)(2,1)}, bf16[2,2,256,128]{3,2,1,0:T(8,128)(2,1)S(1)}, u32[]{:S(2)}, u32[]{:S(2)}) %collective-permute-start.11) | collective-permute-done | bytes 262176 | tf_op jit(solution)/shard_map/ppermute | solution.py:320
  112.0 3.3 %collective-permute-start.10 = (f32[8,128]{1,0:T(8,128)S(1)}, f32[8,128]{1,0:T(8,128)S(1)}, u32[]{:S(2)}, u32[]{:S(2)}) collective-permute-start(f32[8,128]{1,0:T(8,128)S(1)} %add.29), channel_id=1, source_target_pairs={{0,16},{1,17},{2,18},{3,19},{4,20},{5,21},{6,22},{7,23},{8,24},{9,... | collective-permute-start | bytes 12296 | tf_op jit(solution)/shard_map/ppermute | solution.py:320
  115.3 6.3 %collective-permute-done.13.got03 = bf16[2,2,256,128]{3,2,1,0:T(8,128)(2,1)S(1)} collective-permute-done((bf16[2,2,256,128]{3,2,1,0:T(8,128)(2,1)}, bf16[2,2,256,128]{3,2,1,0:T(8,128)(2,1)S(1)}, u32[]{:S(2)}, u32[]{:S(2)}) %collective-permute-start.13) | collective-permute-done | bytes 262176 | tf_op jit(solution)/shard_map/ppermute | solution.py:320
  122.3 1.1 copy-done.4
  125.4 1.3 collective-permute-start.14
  126.7 1.3 collective-permute-start.15
  128.6 1.3 collective-permute-start.17
  129.9 1.3 collective-permute-start.18
  131.3 2.1 %rows.1 = (bf16[128,4096]{1,0:T(8,128)(2,1)}, bf16[128,4096]{1,0:T(8,128)(2,1)}) custom-call(s32[3]{0:T(128)S(1)} %copy-done.12, bf16[128,1024]{1,0:T(8,128)(2,1)S(1)} %copy-done.7, bf16[128,1024]{1,0:T(8,128)(2,1)S(1)} %copy-done.5, bf16[128,1024]{1,0:T(8,128)(2,1)S(1)} %copy-done.8, bf16[128,1024]{1,0:T(8,128)(2,1)S(1)} %copy-done.6, ...), custom_call_target="tpu_custom_call" | custom-call | tf_op jit(solution)/shard_map/rows/pallas_call | solution.py:232
  133.4 2.0 %collective-permute-done.15.refs_2_ = bf16[2,256,128]{2,1,0:T(8,128)(2,1)S(1)} collective-permute-done((bf16[2,256,128]{2,1,0:T(8,128)(2,1)S(1)}, bf16[2,256,128]{2,1,0:T(8,128)(2,1)S(1)}, u32[]{:S(2)}, u32[]{:S(2)}) %collective-permute-start.15) | collective-permute-done | bytes 131104 | tf_op jit(solution)/shard_map/ppermute | solution.py:320
  135.4 1.3 collective-permute-done.17.refs_4_
  136.7 2.9 %collective-permute-done.18.refs_5_ = bf16[2,256,128]{2,1,0:T(8,128)(2,1)S(1)} collective-permute-done((bf16[2,256,128]{2,1,0:T(8,128)(2,1)S(1)}, bf16[2,256,128]{2,1,0:T(8,128)(2,1)S(1)}, u32[]{:S(2)}, u32[]{:S(2)}) %collective-permute-start.18) | collective-permute-done | bytes 131104 | tf_op jit(solution)/shard_map/ppermute | solution.py:320
  139.7 1.3 final.1
  (83 shorter events, 13.7 us)
Async XLA Ops:
  4.1 2.5 %collective-permute-start.2 = (bf16[2,272,128]{2,1,0:T(8,128)(2,1)S(1)}, bf16[2,272,128]{2,1,0:T(8,128)(2,1)S(1)}, u32[]{:S(2)}, u32[]{:S(2)}) collective-permute-start(bf16[2,272,128]{2,1,0:T(8,128)(2,1)S(1)} %get-tuple-element.55), channel_id=1, source_target_pairs={{0,1},{1,0},{2,3},{3,2},{4,5},{5,4},{6,7},{7,6},{8,9},{9,8},{10,11... | collective-permute-start | bytes 417800 | tf_op jit(solution)/shard_map/ppermute | solution.py:320
  6.6 32.1 %copy-start = (bf16[2,2,272,128]{3,2,1,0:T(8,128)(2,1)}, bf16[2,2,272,128]{3,2,1,0:T(8,128)(2,1)S(1)}, u32[]{:S(2)}) copy-start(bf16[2,2,272,128]{3,2,1,0:T(8,128)(2,1)S(1)} %pad_maximum_fusion.own_ref) | copy-start | bytes 835588
  6.7 10.6 %collective-permute-start.3 = (bf16[2,2,272,128]{3,2,1,0:T(8,128)(2,1)S(1)}, bf16[2,2,272,128]{3,2,1,0:T(8,128)(2,1)S(1)}, u32[]{:S(2)}, u32[]{:S(2)}) collective-permute-start(bf16[2,2,272,128]{3,2,1,0:T(8,128)(2,1)S(1)} %pad_maximum_fusion.own_ref), channel_id=1, source_target_pairs={{0,8},{1,9},{2,10},{3,11},{4,12},{5,13},{6,14},{7,15},{8,16},{9,17... | collective-permute-start | bytes 835592 | tf_op jit(solution)/shard_map/ppermute | solution.py:320
  17.3 21.4 %copy-start.1 = (bf16[2,2,272,128]{3,2,1,0:T(8,128)(2,1)}, bf16[2,2,272,128]{3,2,1,0:T(8,128)(2,1)S(1)}, u32[]{:S(2)}) copy-start(bf16[2,2,272,128]{3,2,1,0:T(8,128)(2,1)S(1)} %collective-permute-done.3.za_ref) | copy-start | bytes 835588
  18.6 4.2 %collective-permute-start.5 = (f32[8,128]{1,0:T(8,128)S(1)}, f32[8,128]{1,0:T(8,128)S(1)}, u32[]{:S(2)}, u32[]{:S(2)}) collective-permute-start(f32[8,128]{1,0:T(8,128)S(1)} %broadcast_in_dim.28), channel_id=1, source_target_pairs={{0,32},{32,0},{64,96},{96,64},{1,33},{33,1},{65,97},{97,65},{2,34}... | collective-permute-start | bytes 12296 | tf_op jit(solution)/shard_map/ppermute | solution.py:341
  19.9 8.3 %collective-permute-start.4 = (bf16[2,2,272,128]{3,2,1,0:T(8,128)(2,1)S(1)}, bf16[2,2,272,128]{3,2,1,0:T(8,128)(2,1)S(1)}, u32[]{:S(2)}, u32[]{:S(2)}) collective-permute-start(bf16[2,2,272,128]{3,2,1,0:T(8,128)(2,1)S(1)} %pad_maximum_fusion.own_ref), channel_id=1, source_target_pairs={{0,16},{1,17},{2,18},{3,19},{4,20},{5,21},{6,22},{7,23},{8,24},{9,... | collective-permute-start | bytes 835592 | tf_op jit(solution)/shard_map/ppermute | solution.py:320
  23.4 4.0 %collective-permute-start.6 = (f32[8,128]{1,0:T(8,128)S(1)}, f32[8,128]{1,0:T(8,128)S(1)}, u32[]{:S(2)}, u32[]{:S(2)}) collective-permute-start(f32[8,128]{1,0:T(8,128)S(1)} %broadcast_add_fusion), channel_id=1, source_target_pairs={{0,64},{32,96},{64,0},{96,32},{1,65},{33,97},{65,1},{97,33},{2,66}... | collective-permute-start | bytes 12296 | tf_op jit(solution)/shard_map/ppermute | solution.py:341
  26.0 12.7 %copy-start.11 = (s32[3]{0:T(128)}, s32[3]{0:T(128)S(1)}, u32[]{:S(2)}) copy-start(s32[3]{0:T(128)S(1)} %pad_add_fusion.s_ref) | copy-start | bytes 40
  28.2 10.6 %copy-start.2 = (bf16[2,2,272,128]{3,2,1,0:T(8,128)(2,1)}, bf16[2,2,272,128]{3,2,1,0:T(8,128)(2,1)S(1)}, u32[]{:S(2)}) copy-start(bf16[2,2,272,128]{3,2,1,0:T(8,128)(2,1)S(1)} %collective-permute-done.4.zc_ref) | copy-start | bytes 835588
  29.8 16.5 %all-to-all-start.1 = ((bf16[4,2,2,272,128]{4,3,2,1,0:T(8,128)(2,1)}), bf16[4,2,2,272,128]{4,3,2,1,0:T(8,128)(2,1)S(1)}, u32[]{:S(2)}, u32[]{:S(2)}) async-start(bf16[4,2,2,272,128]{4,3,2,1,0:T(8,128)(2,1)} %spread.3), calls=%async_computation.1 | async-start | bytes 2228224 | tf_op jit(solution)/shard_map/all_to_all | solution.py:325
  35.2 15.9 %collective-permute-start.1 = (bf16[128,2048]{1,0:T(8,128)(2,1)S(1)}, bf16[128,2048]{1,0:T(8,128)(2,1)}, u32[]{:S(2)}, u32[]{:S(2)}) collective-permute-start(bf16[128,2048]{1,0:T(8,128)(2,1)S(1)} %dynamic-slice_bitcast_fusion), channel_id=1, source_target_pairs={{0,1},{1,0},{2,3},{3,2},{4,5},{5,4},{6,7},{7,6},{8,9},{9,8},{10,11... | collective-permute-start | bytes 1572872 | tf_op jit(solution)/shard_map/ppermute | solution.py:320
  38.5 12.6 %collective-permute-start = (bf16[128,2048]{1,0:T(8,128)(2,1)S(1)}, bf16[128,2048]{1,0:T(8,128)(2,1)}, u32[]{:S(2)}, u32[]{:S(2)}) collective-permute-start(bf16[128,2048]{1,0:T(8,128)(2,1)S(1)} %dynamic-slice_bitcast_fusion.1), channel_id=1, source_target_pairs={{0,1},{1,0},{2,3},{3,2},{4,5},{5,4},{6,7},{7,6},{8,9},{9,8},{10,11... | collective-permute-start | bytes 1572872 | tf_op jit(solution)/shard_map/ppermute | solution.py:320
  47.4 23.9 %all-to-all-start = ((bf16[4,2,2,272,128]{4,3,2,1,0:T(8,128)(2,1)}), bf16[4,2,2,272,128]{4,3,2,1,0:T(8,128)(2,1)S(1)}, u32[]{:S(2)}, u32[]{:S(2)}) async-start(bf16[4,2,2,272,128]{4,3,2,1,0:T(8,128)(2,1)} %spread.2), calls=%async_computation | async-start | bytes 2228224 | tf_op jit(solution)/shard_map/all_to_all | solution.py:325
  71.3 51.1 %all-to-all-start.2 = ((bf16[4,2,2,256,128]{4,3,2,1,0:T(8,128)(2,1)}), bf16[4,2,2,256,128]{4,3,2,1,0:T(8,128)(2,1)S(1)}, u32[]{:S(2)}, u32[]{:S(2)}) async-start(bf16[4,2,2,256,128]{4,3,2,1,0:T(8,128)(2,1)} %get-tuple-element.40), calls=%async_computation.2 | async-start | bytes 2097152 | tf_op jit(solution)/shard_map/all_to_all | solution.py:325
  75.3 27.1 %copy-start.17 = (f32[8,128]{1,0:T(8,128)S(1)}, f32[8,128]{1,0:T(8,128)}, u32[]{:S(2)}) copy-start(f32[8,128]{1,0:T(8,128)} %get-tuple-element.33) | copy-start | bytes 12292
  75.3 47.0 %copy-start.3 = (f32[3,2,256,128]{3,2,1,0:T(8,128)S(1)}, f32[3,2,256,128]{3,2,1,0:T(8,128)}, u32[]{:S(2)}) copy-start(f32[3,2,256,128]{3,2,1,0:T(8,128)} %get-tuple-element.41.loc1) | copy-start | bytes 2359300
  75.3 47.0 %copy-start.12 = (s32[3]{0:T(128)S(1)}, s32[3]{0:T(128)}, u32[]{:S(2)}) copy-start(s32[3]{0:T(128)} %copy-done.11) | copy-start | bytes 40
  97.3 31.4 %collective-permute-start.7 = (bf16[2,128,1024]{2,1,0:T(8,128)(2,1)}, bf16[2,128,1024]{2,1,0:T(8,128)(2,1)S(1)}, u32[]{:S(2)}, u32[]{:S(2)}) collective-permute-start(bf16[2,128,1024]{2,1,0:T(8,128)(2,1)} %get-tuple-element.31), channel_id=1, source_target_pairs={{0,1},{1,0},{2,3},{3,2},{4,5},{5,4},{6,7},{7,6},{8,9},{9,8},{10,11... | collective-permute-start | bytes 1572872 | tf_op jit(solution)/shard_map/ppermute | solution.py:320
  102.3 27.7 %collective-permute-start.8 = (bf16[2,128,1024]{2,1,0:T(8,128)(2,1)}, bf16[2,128,1024]{2,1,0:T(8,128)(2,1)S(1)}, u32[]{:S(2)}, u32[]{:S(2)}) collective-permute-start(bf16[2,128,1024]{2,1,0:T(8,128)(2,1)} %get-tuple-element.32), channel_id=1, source_target_pairs={{0,1},{1,0},{2,3},{3,2},{4,5},{5,4},{6,7},{7,6},{8,9},{9,8},{10,11... | collective-permute-start | bytes 1572872 | tf_op jit(solution)/shard_map/ppermute | solution.py:320
  102.4 4.3 %collective-permute-start.9 = (f32[8,128]{1,0:T(8,128)S(1)}, f32[8,128]{1,0:T(8,128)S(1)}, u32[]{:S(2)}, u32[]{:S(2)}) collective-permute-start(f32[8,128]{1,0:T(8,128)S(1)} %copy-done.17), channel_id=1, source_target_pairs={{0,8},{1,9},{2,10},{3,11},{4,12},{5,13},{6,14},{7,15},{8,0},{9,1},... | collective-permute-start | bytes 12296 | tf_op jit(solution)/shard_map/ppermute | solution.py:320
  103.1 8.9 %collective-permute-start.11 = (bf16[2,2,256,128]{3,2,1,0:T(8,128)(2,1)}, bf16[2,2,256,128]{3,2,1,0:T(8,128)(2,1)S(1)}, u32[]{:S(2)}, u32[]{:S(2)}) collective-permute-start(bf16[2,2,256,128]{3,2,1,0:T(8,128)(2,1)} %get-tuple-element.36), channel_id=1, source_target_pairs={{0,6},{1,7},{2,0},{3,1},{4,2},{5,3},{6,4},{7,5},{8,14},{9,15},{10,... | collective-permute-start | bytes 786440 | tf_op jit(solution)/shard_map/ppermute | solution.py:320
  106.0 9.3 %collective-permute-start.12 = (bf16[2,2,256,128]{3,2,1,0:T(8,128)(2,1)}, bf16[2,2,256,128]{3,2,1,0:T(8,128)(2,1)S(1)}, u32[]{:S(2)}, u32[]{:S(2)}) collective-permute-start(bf16[2,2,256,128]{3,2,1,0:T(8,128)(2,1)} %get-tuple-element.37), channel_id=1, source_target_pairs={{0,4},{1,5},{2,6},{3,7},{4,0},{5,1},{6,2},{7,3},{8,12},{9,13},{10,... | collective-permute-start | bytes 786440 | tf_op jit(solution)/shard_map/ppermute | solution.py:320
  106.6 15.0 %collective-permute-start.13 = (bf16[2,2,256,128]{3,2,1,0:T(8,128)(2,1)}, bf16[2,2,256,128]{3,2,1,0:T(8,128)(2,1)S(1)}, u32[]{:S(2)}, u32[]{:S(2)}) collective-permute-start(bf16[2,2,256,128]{3,2,1,0:T(8,128)(2,1)} %get-tuple-element.38), channel_id=1, source_target_pairs={{0,2},{1,3},{2,4},{3,5},{4,6},{5,7},{6,0},{7,1},{8,10},{9,11},{10,... | collective-permute-start | bytes 786440 | tf_op jit(solution)/shard_map/ppermute | solution.py:320
  112.0 16.0 %collective-permute-start.10 = (f32[8,128]{1,0:T(8,128)S(1)}, f32[8,128]{1,0:T(8,128)S(1)}, u32[]{:S(2)}, u32[]{:S(2)}) collective-permute-start(f32[8,128]{1,0:T(8,128)S(1)} %add.29), channel_id=1, source_target_pairs={{0,16},{1,17},{2,18},{3,19},{4,20},{5,21},{6,22},{7,23},{8,24},{9,... | collective-permute-start | bytes 12296 | tf_op jit(solution)/shard_map/ppermute | solution.py:320
  124.4 6.9 %copy-start.6 = (bf16[128,1024]{1,0:T(8,128)(2,1)S(1)}, bf16[128,1024]{1,0:T(8,128)(2,1)}, u32[]{:S(2)}) copy-start(bf16[128,1024]{1,0:T(8,128)(2,1)} %get-tuple-element.30.dq1) | copy-start | bytes 786436
  124.4 6.9 %copy-start.7 = (bf16[128,1024]{1,0:T(8,128)(2,1)S(1)}, bf16[128,1024]{1,0:T(8,128)(2,1)}, u32[]{:S(2)}) copy-start(bf16[128,1024]{1,0:T(8,128)(2,1)} %get-tuple-element.27.oo0) | copy-start | bytes 786436
  124.4 6.9 %copy-start.8 = (bf16[128,1024]{1,0:T(8,128)(2,1)S(1)}, bf16[128,1024]{1,0:T(8,128)(2,1)}, u32[]{:S(2)}) copy-start(bf16[128,1024]{1,0:T(8,128)(2,1)} %get-tuple-element.29.dq0) | copy-start | bytes 786436
  125.4 7.9 %collective-permute-start.14 = (bf16[2,256,128]{2,1,0:T(8,128)(2,1)S(1)}, bf16[2,256,128]{2,1,0:T(8,128)(2,1)S(1)}, u32[]{:S(2)}, u32[]{:S(2)}) collective-permute-start(bf16[2,256,128]{2,1,0:T(8,128)(2,1)S(1)} %get-tuple-element.43), channel_id=1, source_target_pairs={{8,0},{9,1},{10,2},{11,3},{12,4},{13,5},{14,6},{15,7},{16,8},{17,9... | collective-permute-start | bytes 393224 | tf_op jit(solution)/shard_map/ppermute | solution.py:320
  126.7 8.7 %collective-permute-start.15 = (bf16[2,256,128]{2,1,0:T(8,128)(2,1)S(1)}, bf16[2,256,128]{2,1,0:T(8,128)(2,1)S(1)}, u32[]{:S(2)}, u32[]{:S(2)}) collective-permute-start(bf16[2,256,128]{2,1,0:T(8,128)(2,1)S(1)} %get-tuple-element.44), channel_id=1, source_target_pairs={{16,0},{17,1},{18,2},{19,3},{20,4},{21,5},{22,6},{23,7},{24,8},{25... | collective-permute-start | bytes 393224 | tf_op jit(solution)/shard_map/ppermute | solution.py:320
  128.0 7.4 %collective-permute-start.16 = (bf16[2,256,128]{2,1,0:T(8,128)(2,1)S(1)}, bf16[2,256,128]{2,1,0:T(8,128)(2,1)S(1)}, u32[]{:S(2)}, u32[]{:S(2)}) collective-permute-start(bf16[2,256,128]{2,1,0:T(8,128)(2,1)S(1)} %get-tuple-element.45), channel_id=1, source_target_pairs={{0,1},{1,0},{2,3},{3,2},{4,5},{5,4},{6,7},{7,6},{8,9},{9,8},{10,11... | collective-permute-start | bytes 393224 | tf_op jit(solution)/shard_map/ppermute | solution.py:320
  128.6 8.1 %collective-permute-start.17 = (bf16[2,256,128]{2,1,0:T(8,128)(2,1)S(1)}, bf16[2,256,128]{2,1,0:T(8,128)(2,1)S(1)}, u32[]{:S(2)}, u32[]{:S(2)}) collective-permute-start(bf16[2,256,128]{2,1,0:T(8,128)(2,1)S(1)} %get-tuple-element.46), channel_id=1, source_target_pairs={{8,1},{9,0},{10,3},{11,2},{12,5},{13,4},{14,7},{15,6},{16,9},{17,8... | collective-permute-start | bytes 393224 | tf_op jit(solution)/shard_map/ppermute | solution.py:320
  129.9 9.7 %collective-permute-start.18 = (bf16[2,256,128]{2,1,0:T(8,128)(2,1)S(1)}, bf16[2,256,128]{2,1,0:T(8,128)(2,1)S(1)}, u32[]{:S(2)}, u32[]{:S(2)}) collective-permute-start(bf16[2,256,128]{2,1,0:T(8,128)(2,1)S(1)} %get-tuple-element.47), channel_id=1, source_target_pairs={{16,1},{17,0},{18,3},{19,2},{20,5},{21,4},{22,7},{23,6},{24,9},{25... | collective-permute-start | bytes 393224 | tf_op jit(solution)/shard_map/ppermute | solution.py:320
  (8 other events, 20.8 us)
